TPU v7x, 256 devices: a whole 4x4x8 slice. The times are simulated.
256 devices in a mesh: seq: 8 (over y_hi, x), chan: 32 (over z, y_lo, core).
Axes of the slice: x: 4, y: 4 (y_hi: 2, y_lo: 2; y = y_hi * 2 + y_lo), z: 8, core: 2. Of those that a mesh axis runs over, the one named last changes fastest.
Arguments:
- tokens: bfloat16 [1024, 8192], P('seq', 'chan'), may hold values from -11 to 11
- norm_gain: bfloat16 [8192], P('chan'), may hold values from 0.099609375 to 1.8984375
- in_weight: bfloat16 [8192, 3, 4096], P(None, None, 'chan'), may hold values from -0.0625 to 0.0625
- short_filter: float32 [3, 3, 4096], P(None, None, 'chan'), may hold values from -3 to 3
- prior_rows: bfloat16 [2, 3, 4096], P(None, None, 'chan'), may hold values from -5 to 5
- decay_rate: float32 [4096, 16], P('chan'), may hold values from 0.0001953125 to 0.05
- pole_angle: float32 [4096, 16], P('chan'), may hold values from -3.140625 to 3.140625
- residue: float32 [2, 4096, 16], P(None, 'chan'), may hold values from -0.32 to 0.32
- prior_state: float32 [2, 4096, 16], P(None, 'chan'), may hold values from -202.38577 to 202.38577
- skip_weight: float32 [4096], P('chan'), may hold values from -3 to 3
- out_weight: bfloat16 [4096, 8192], P(None, 'chan'), may hold values from -0.09375 to 0.09375
Outputs:
- mixed: bfloat16 [1024, 8192], P('seq', 'chan')
All inputs are finite; a program needn't handle non-finite values.
Results may differ from a plain program's by a relative error of at most 0.0083.
Values may be sent and summed in bfloat16 or wider, within the bound.
A program may use at most 64 MiB of HBM per device.

v0:
```python
import math

import jax
import jax.numpy as jnp
from jax import lax
from jax.sharding import PartitionSpec as P

D = 8192
SHORT = 3


EPSILON = 1e-06
HIGHEST = lax.Precision.HIGHEST


def passed_along(x, axis, by):
    count = lax.axis_size(axis)
    pairs = [(i, i + by) for i in range(count) if 0 <= i + by < count]
    return lax.ppermute(x, axis, pairs)


def complex_product(first, second):
    real_part = first[0] * second[0] - first[1] * second[1]
    imaginary_part = first[0] * second[1] + first[1] * second[0]
    return jnp.stack([real_part, imaginary_part])


def powers(rate, angle, counts):
    magnitude = jnp.exp(-counts[:, None, None] * rate[None])
    phase = counts[:, None, None] * angle[None]
    return jnp.stack([magnitude * jnp.cos(phase), magnitude * jnp.sin(phase)])


def body(
    tokens,
    norm_gain,
    in_weight,
    short_filter,
    prior_rows,
    decay_rate,
    pole_angle,
    residue,
    prior_state,
    skip_weight,
    out_weight,
):
    length = tokens.shape[0]
    local_chans = in_weight.shape[2]
    width = 3 * local_chans
    in_matrix = in_weight.reshape(in_weight.shape[0], width)
    values = tokens.astype(jnp.float32)
    position = lax.axis_index("seq")
    squares = lax.psum(jnp.sum(values * values, axis=1), "chan")
    scale = lax.rsqrt(squares / D + EPSILON)
    normed = (values * scale[:, None] * norm_gain.astype(jnp.float32)[None, :]).astype(jnp.bfloat16)
    rows = in_matrix
    projected = jnp.dot(
        lax.all_gather(normed, "chan", axis=1, tiled=True), rows, preferred_element_type=jnp.float32
    )
    projected = projected.astype(jnp.bfloat16)
    margin = SHORT - 1
    rim = passed_along(projected[length - margin :], "seq", 1)
    rim = jnp.where(position == 0, prior_rows.reshape(margin, width), rim)
    extended = jnp.concatenate([rim, projected], axis=0).astype(jnp.float32)
    taps = short_filter.reshape(SHORT, width)
    convolved = jnp.zeros((length, width), jnp.float32)
    for lag in range(SHORT):
        convolved = convolved + taps[lag][None, :] * extended[margin - lag : margin - lag + length]
    convolved = convolved.reshape(length, 3, local_chans)
    query_rows = convolved[:, 0, :]
    drive = convolved[:, 1, :] * convolved[:, 2, :]
    block = math.gcd(64, length)
    blocks = length // block
    table = powers(decay_rate, pole_angle, jnp.arange(block + 1, dtype=jnp.float32))
    response = jnp.sum(
        table[0, :block] * residue[0][None] - table[1, :block] * residue[1][None], axis=2
    )
    offsets = jnp.arange(block)[:, None] - jnp.arange(block)[None, :]
    toeplitz = jnp.where((offsets >= 0)[:, :, None], response[jnp.clip(offsets, 0, block - 1)], 0.0)
    drive_blocks = drive.reshape(blocks, block, local_chans)
    inner = jnp.einsum("tsc,bsc->btc", toeplitz, drive_blocks, precision=HIGHEST)
    reverse = table[:, :block][:, ::-1]
    ends = jnp.einsum("bsc,rscm->brcm", drive_blocks, reverse, precision=HIGHEST)
    step_power = table[:, block]

    def advance(carry, end):
        return (complex_product(step_power, carry) + end, carry)

    final, starts = lax.scan(advance, jnp.zeros_like(prior_state), ends)
    shard_power = powers(decay_rate, pole_angle, jnp.full((1,), float(length), jnp.float32))[:, 0]
    incoming = jnp.where(position == 0, prior_state, 0.0)
    for hop in range(lax.axis_size("seq") - 1):
        sent = passed_along(complex_product(shard_power, incoming) + final, "seq", 1)
        incoming = jnp.where(position == hop + 1, sent, incoming)
    start_powers = powers(decay_rate, pole_angle, jnp.arange(blocks, dtype=jnp.float32) * block)
    block_states = complex_product(start_powers, incoming[:, None]) + jnp.moveaxis(starts, 0, 1)
    lifted = complex_product(residue[:, None], table[:, 1:])
    from_state = jnp.einsum(
        "tcm,bcm->btc", lifted[0], block_states[0], precision=HIGHEST
    ) - jnp.einsum("tcm,bcm->btc", lifted[1], block_states[1], precision=HIGHEST)
    mode_out = (inner + from_state).reshape(length, local_chans)
    gated = (query_rows * (mode_out + skip_weight[None, :] * drive)).astype(jnp.bfloat16)
    rows = out_weight
    summed = jnp.dot(
        lax.all_gather(gated, "chan", axis=1, tiled=True), rows, preferred_element_type=jnp.float32
    )
    return (values + summed).astype(jnp.bfloat16)


def solution(mesh):
    return jax.shard_map(
        body,
        mesh=mesh,
        in_specs=(
            P("seq", "chan"),
            P("chan"),
            P(None, None, "chan"),
            P(None, None, "chan"),
            P(None, None, "chan"),
            P("chan", None),
            P("chan", None),
            P(None, "chan", None),
            P(None, "chan", None),
            P("chan"),
            P(None, "chan"),
        ),
        out_specs=P("seq", "chan"),
        check_vma=False,
    )
```

profile of v0, /device:TPU:25, one launch (start us, length us, event | category | flops | bytes accessed | tf_op | source)
XLA Modules:
  0.0 339.3 jit_solution(12411156010365411920)
XLA Ops:
  8.3 52.2 %psum.7 = f32[128]{0:T(128)S(1)} all-reduce(f32[128]{0:T(128)S(1)} %fusion.19), channel_id=1, replica_groups=mesh['seq'=8,'chan'=32] {'chan'}, use_global_device_ids=true, to_apply=%region_1.0 | all-reduce | flops 128 | bytes 1024 | tf_op jit(solution)/shard_map/psum | solution.py:53
  60.5 1.6 fusion.21
  62.2 8.7 %copy.53 = bf16[8192,3,128]{0,2,1:T(8,128)(2,1)} copy(bf16[8192,3,128]{2,0,1:T(8,128)(2,1)} %param.15) | data formatting | bytes 12582912 | tf_op args[2]
  70.9 2.6 fusion.17
  73.6 2.6 fusion.18
  78.6 54.0 %all-gather.3.cloned.1.call-done = bf16[128,8192]{1,0:T(8,128)(2,1)} async-done(((bf16[128,256]{1,0:T(8,128)(2,1)}), bf16[128,8192]{1,0:T(8,128)(2,1)}) %all-gather.3.cloned.1.call-update) | async-done | bytes 2097168 | tf_op jit(solution)/shard_map/all_gather | solution.py:58
  132.5 5.4 %convolution_convert_fusion = bf16[128,384]{1,0:T(8,128)(2,1)S(1)} fusion(bf16[128,8192]{1,0:T(8,128)(2,1)} %all-gather.3.cloned.1.call-done, bf16[8192,384]{0,1:T(8,128)(2,1)} %bitcast.192), kind=kOutput, calls=%fused_computation.11 | convolution fusion | flops 805355520 | bytes 8486912 | tf_op jit(solution)/shard_map/dot_general | solution.py:57
  137.9 3.3 collective-permute-start
  141.3 2.3 rev.3
  143.5 4.1 %copy.62 = f32[2,64,128,16]{1,3,0,2:T(8,128)} copy(f32[2,64,128,16]{2,3,0,1:T(8,128)} %rev.3) | data formatting | bytes 2097152 | tf_op jit(solution)/shard_map/rev | solution.py:82
  148.8 17.0 %convolution_bitcast_fusion = f32[2,2,128,16]{3,0,1,2:T(2,128)} fusion(f32[2,64,128,16]{1,3,0,2:T(8,128)} %copy.62, f32[2,64,128,1]{1,0,3,2:T(2,128)} %copy.71), kind=kOutput, calls=%fused_computation.10 | convolution fusion | flops 6291456 | bytes 1146880 | tf_op jit(solution)/shard_map/bsc,rscm->brcm/dot_general | solution.py:83
  168.9 3.1 collective-permute-start.1
  172.0 5.0 %collective-permute-done.1 = f32[2,128,16]{1,2,0:T(8,128)S(1)} collective-permute-done((f32[2,128,16]{1,2,0:T(8,128)S(1)}, f32[2,128,16]{1,2,0:T(8,128)S(1)}, u32[]{:S(2)}, u32[]{:S(2)}) %collective-permute-start.1) | collective-permute-done | bytes 16416 | tf_op jit(solution)/shard_map/ppermute | solution.py:19
  177.0 1.9 collective-permute-start.2
  179.6 5.4 %collective-permute-done.2 = f32[2,128,16]{1,2,0:T(8,128)S(1)} collective-permute-done((f32[2,128,16]{1,2,0:T(8,128)S(1)}, f32[2,128,16]{1,2,0:T(8,128)S(1)}, u32[]{:S(2)}, u32[]{:S(2)}) %collective-permute-start.2) | collective-permute-done | bytes 16416 | tf_op jit(solution)/shard_map/ppermute | solution.py:19
  185.7 1.9 collective-permute-start.3
  187.6 2.3 multiply_add_fusion.1
  190.0 4.0 %collective-permute-done.3 = f32[2,128,16]{1,2,0:T(8,128)S(1)} collective-permute-done((f32[2,128,16]{1,2,0:T(8,128)}, f32[2,128,16]{1,2,0:T(8,128)S(1)}, u32[]{:S(2)}, u32[]{:S(2)}) %collective-permute-start.3) | collective-permute-done | bytes 16416 | tf_op jit(solution)/shard_map/ppermute | solution.py:19
  194.0 1.9 collective-permute-start.4
  196.0 6.1 %collective-permute-done.4 = f32[2,128,16]{1,2,0:T(8,128)S(1)} collective-permute-done((f32[2,128,16]{1,2,0:T(8,128)S(1)}, f32[2,128,16]{1,2,0:T(8,128)S(1)}, u32[]{:S(2)}, u32[]{:S(2)}) %collective-permute-start.4) | collective-permute-done | bytes 16416 | tf_op jit(solution)/shard_map/ppermute | solution.py:19
  202.1 1.9 collective-permute-start.5
  204.1 6.2 %collective-permute-done.5 = f32[2,128,16]{1,2,0:T(8,128)S(1)} collective-permute-done((f32[2,128,16]{1,2,0:T(8,128)S(1)}, f32[2,128,16]{1,2,0:T(8,128)S(1)}, u32[]{:S(2)}, u32[]{:S(2)}) %collective-permute-start.5) | collective-permute-done | bytes 16416 | tf_op jit(solution)/shard_map/ppermute | solution.py:19
  210.3 1.9 collective-permute-start.6
  212.8 5.6 %collective-permute-done.6 = f32[2,128,16]{1,2,0:T(8,128)S(1)} collective-permute-done((f32[2,128,16]{1,2,0:T(8,128)S(1)}, f32[2,128,16]{1,2,0:T(8,128)S(1)}, u32[]{:S(2)}, u32[]{:S(2)}) %collective-permute-start.6) | collective-permute-done | bytes 16416 | tf_op jit(solution)/shard_map/ppermute | solution.py:19
  219.0 2.1 collective-permute-start.7
  221.7 2.5 copy.67
  224.2 1.6 copy.68
  225.7 14.1 %gather_fusion = f32[4096,128]{1,0:T(8,128)} fusion(f32[64,128]{1,0:T(8,128)S(1)} %get-tuple-element.87, s32[4096]{0:T(1024)S(1)} %broadcast_clamp_fusion), kind=kCustom, calls=%fused_computation | custom fusion | bytes 4210688 | tf_op jit(solution)/shard_map/gather | solution.py:79
  239.8 5.6 %copy.59 = f32[64,64,128]{1,0,2:T(8,128)} copy(f32[64,64,128]{2,1,0:T(8,128)} %bitcast.193) | data formatting | bytes 4194304 | tf_op jit(solution)/shard_map/gather | solution.py:79
  252.2 8.4 %fusion.7 = f32[2,64,128]{1,0,2:T(2,128)S(1)} fusion(f32[128,2,64]{2,1,0:T(2,128)S(1)} %convolution_subtract_fusion, f32[2,64,128]{1,0,2:T(2,128)S(1)} %copy-done.6, f32[64,64,128]{1,0,2:T(8,128)} %copy.59, pred[64,64]{1,0:T(8,128)(4,1)} %subtract_compare_fusion), kind=kOutput, calls=%fused_computation.13 | convolution fusion | flops 13123584 | bytes 2297856 | tf_op jit(solution)/shard_map/tsc,bsc->btc/dot_general | solution.py:81
  261.5 68.5 %all-gather.5.cloned.1.call-done = bf16[128,4096]{0,1:T(8,128)(2,1)} async-done(((bf16[128,128]{0,1:T(8,128)(2,1)}), bf16[128,4096]{0,1:T(8,128)(2,1)}) %all-gather.5.cloned.1.call-update) | async-done | bytes 1048592 | tf_op jit(solution)/shard_map/all_gather | solution.py:105
  330.0 2.4 fusion.10
  (100 shorter events, 20.5 us)
Async XLA Ops:
  6.5 323.5 %copy-start = (bf16[4096,256]{1,0:T(8,128)(2,1)S(1)}, bf16[4096,256]{1,0:T(8,128)(2,1)}, u32[]{:S(2)}) copy-start(bf16[4096,256]{1,0:T(8,128)(2,1)} %param.23) | copy-start | bytes 6291460
  6.5 126.0 %all-gather.3.cloned.1.call-start = ((), (), s32[]{:S(2)}) async-start(), calls=%async_computation | async-start | bytes 2162688 | tf_op jit(solution)/shard_map/all_gather | solution.py:58
  62.1 267.9 %all-gather.5.cloned.1.call-start = ((), (), s32[]{:S(2)}) async-start(), calls=%async_computation.1 | async-start | bytes 1081344 | tf_op jit(solution)/shard_map/all_gather | solution.py:105
  62.2 8.7 %copy-start.7 = (f32[128,16]{0,1:T(8,128)S(1)}, f32[128,16]{0,1:T(8,128)}, u32[]{:S(2)}) copy-start(f32[128,16]{0,1:T(8,128)} %param.19) | copy-start | bytes 24580
  62.2 8.7 %copy-start.8 = (f32[128,16]{0,1:T(8,128)S(1)}, f32[128,16]{0,1:T(8,128)}, u32[]{:S(2)}) copy-start(f32[128,16]{0,1:T(8,128)} %param.18) | copy-start | bytes 24580
  70.9 6.4 %copy-start.11 = (f32[3,3,128]{2,1,0:T(4,128)S(1)}, f32[3,3,128]{2,1,0:T(4,128)}, u32[]{:S(2)}) copy-start(f32[3,3,128]{2,1,0:T(4,128)} %param.16) | copy-start | bytes 13828
  70.9 6.4 %copy-start.9 = (f32[2,128,16]{1,2,0:T(8,128)S(1)}, f32[2,128,16]{1,2,0:T(8,128)}, u32[]{:S(2)}) copy-start(f32[2,128,16]{1,2,0:T(8,128)} %param.21) | copy-start | bytes 49156
  137.9 9.7 %collective-permute-start = (bf16[2,384]{1,0:T(2,128)(2,1)S(1)}, bf16[2,384]{1,0:T(2,128)(2,1)S(1)}, u32[]{:S(2)}, u32[]{:S(2)}) collective-permute-start(bf16[2,384]{1,0:T(2,128)(2,1)S(1)} %slice.232), channel_id=1, source_target_pairs={{0,32},{32,64},{64,96},{96,128},{128,160},{160,192},{192,224},{1,3... | collective-permute-start | bytes 4616 | tf_op jit(solution)/shard_map/ppermute | solution.py:19
  143.5 4.1 %copy-start.12 = (bf16[2,3,128]{2,0,1:T(2,128)(2,1)S(1)}, bf16[2,3,128]{2,0,1:T(2,128)(2,1)}, u32[]{:S(2)}) copy-start(bf16[2,3,128]{2,0,1:T(2,128)(2,1)} %param.17) | copy-start | bytes 4612
  148.8 38.8 %copy-start.1 = (f32[1,65,128,16]{2,3,1,0:T(8,128)S(1)}, f32[1,65,128,16]{2,3,1,0:T(8,128)}, u32[]{:S(2)}) copy-start(f32[1,65,128,16]{2,3,1,0:T(8,128)} %get-tuple-element.105) | copy-start | bytes 1597444
  168.9 8.1 %collective-permute-start.1 = (f32[2,128,16]{1,2,0:T(8,128)S(1)}, f32[2,128,16]{1,2,0:T(8,128)S(1)}, u32[]{:S(2)}, u32[]{:S(2)}) collective-permute-start(f32[2,128,16]{1,2,0:T(8,128)S(1)} %maximum_add_fusion.1), channel_id=1, source_target_pairs={{0,32},{32,64},{64,96},{96,128},{128,160},{160,192},{192,224},{1,3... | collective-permute-start | bytes 49160 | tf_op jit(solution)/shard_map/ppermute | solution.py:19
  177.0 8.1 %collective-permute-start.2 = (f32[2,128,16]{1,2,0:T(8,128)S(1)}, f32[2,128,16]{1,2,0:T(8,128)S(1)}, u32[]{:S(2)}, u32[]{:S(2)}) collective-permute-start(f32[2,128,16]{1,2,0:T(8,128)S(1)} %maximum_add_fusion.2), channel_id=1, source_target_pairs={{0,32},{32,64},{64,96},{96,128},{128,160},{160,192},{192,224},{1,3... | collective-permute-start | bytes 49160 | tf_op jit(solution)/shard_map/ppermute | solution.py:19
  185.7 8.3 %collective-permute-start.3 = (f32[2,128,16]{1,2,0:T(8,128)}, f32[2,128,16]{1,2,0:T(8,128)S(1)}, u32[]{:S(2)}, u32[]{:S(2)}) collective-permute-start(f32[2,128,16]{1,2,0:T(8,128)} %maximum_add_fusion.3), channel_id=1, source_target_pairs={{0,32},{32,64},{64,96},{96,128},{128,160},{160,192},{192,224},{1,3... | collective-permute-start | bytes 49160 | tf_op jit(solution)/shard_map/ppermute | solution.py:19
  190.0 34.2 %copy-start.4 = (f32[64,128,16]{1,2,0:T(8,128)S(1)}, f32[64,128,16]{1,2,0:T(8,128)}, u32[]{:S(2)}) copy-start(f32[64,128,16]{1,2,0:T(8,128)} %get-tuple-element.85) | copy-start | bytes 1572868
  194.0 8.1 %collective-permute-start.4 = (f32[2,128,16]{1,2,0:T(8,128)S(1)}, f32[2,128,16]{1,2,0:T(8,128)S(1)}, u32[]{:S(2)}, u32[]{:S(2)}) collective-permute-start(f32[2,128,16]{1,2,0:T(8,128)S(1)} %maximum_add_fusion.4), channel_id=1, source_target_pairs={{0,32},{32,64},{64,96},{96,128},{128,160},{160,192},{192,224},{1,3... | collective-permute-start | bytes 49160 | tf_op jit(solution)/shard_map/ppermute | solution.py:19
  202.1 8.1 %collective-permute-start.5 = (f32[2,128,16]{1,2,0:T(8,128)S(1)}, f32[2,128,16]{1,2,0:T(8,128)S(1)}, u32[]{:S(2)}, u32[]{:S(2)}) collective-permute-start(f32[2,128,16]{1,2,0:T(8,128)S(1)} %maximum_add_fusion.5), channel_id=1, source_target_pairs={{0,32},{32,64},{64,96},{96,128},{128,160},{160,192},{192,224},{1,3... | collective-permute-start | bytes 49160 | tf_op jit(solution)/shard_map/ppermute | solution.py:19
  210.3 8.1 %collective-permute-start.6 = (f32[2,128,16]{1,2,0:T(8,128)S(1)}, f32[2,128,16]{1,2,0:T(8,128)S(1)}, u32[]{:S(2)}, u32[]{:S(2)}) collective-permute-start(f32[2,128,16]{1,2,0:T(8,128)S(1)} %maximum_add_fusion.6), channel_id=1, source_target_pairs={{0,32},{32,64},{64,96},{96,128},{128,160},{160,192},{192,224},{1,3... | collective-permute-start | bytes 49160 | tf_op jit(solution)/shard_map/ppermute | solution.py:19
  219.0 28.1 %collective-permute-start.7 = (f32[2,128,16]{1,2,0:T(8,128)}, f32[2,128,16]{1,2,0:T(8,128)S(1)}, u32[]{:S(2)}, u32[]{:S(2)}) collective-permute-start(f32[2,128,16]{1,2,0:T(8,128)} %maximum_add_fusion.7), channel_id=1, source_target_pairs={{0,32},{32,64},{64,96},{96,128},{128,160},{160,192},{192,224},{1,3... | collective-permute-start | bytes 49160 | tf_op jit(solution)/shard_map/ppermute | solution.py:19
  239.8 5.6 %copy-start.10 = (f32[2,2,128,16]{2,3,1,0:T(8,128)S(1)}, f32[2,2,128,16]{2,3,1,0:T(8,128)}, u32[]{:S(2)}) copy-start(f32[2,2,128,16]{2,3,1,0:T(8,128)} %get-tuple-element.34) | copy-start | bytes 98308
  245.5 4.6 %copy-start.2 = (f32[64,128,16]{0,2,1:T(8,128)S(1)}, f32[64,128,16]{0,2,1:T(8,128)}, u32[]{:S(2)}) copy-start(f32[64,128,16]{0,2,1:T(8,128)} %copy.67) | copy-start | bytes 1572868
  247.1 5.1 %copy-start.6 = (f32[2,64,128]{1,0,2:T(2,128)S(1)}, f32[2,64,128]{1,0,2:T(2,128)}, u32[]{:S(2)}) copy-start(f32[2,64,128]{1,0,2:T(2,128)} %copy.60) | copy-start | bytes 196612
  248.8 2.3 copy-start.3
  252.1 8.6 %copy-start.13 = (f32[128]{0:T(128)S(1)}, f32[128]{0:T(128)}, u32[]{:S(2)}) copy-start(f32[128]{0:T(128)} %param.22) | copy-start | bytes 1540
  252.1 77.9 %copy-start.5 = (bf16[128,256]{1,0:T(8,128)(2,1)S(1)}, bf16[128,256]{1,0:T(8,128)(2,1)}, u32[]{:S(2)}) copy-start(bf16[128,256]{1,0:T(8,128)(2,1)} %param.13) | copy-start | bytes 196612
Sparse Core Ops, SparseCore 0:
  62.2 70.2 all-gather.2
  261.6 68.3 all-gather.4
where the time goes:
time: 342 us; the launch traced here: 339 us
  waiting for transfers between devices  155 us (45%)
  blocking collectives  52.2 us (15%)
  local copies, waits for them, and re-layouts  44.3 us (13%)
  matrix products  35.3 us (10%)
  other arithmetic  20.8 us (6%)
  starting transfers between devices  18.1 us (5%)
  between operations  13.8 us (4%)
    all_gather x1, waiting for transfers between devices, body(): lax.all_gather(gated, 'chan', axis=1, tiled=True)  68.5 us
    all_gather x1, waiting for transfers between devices, body(): lax.all_gather(normed, 'chan', axis=1, tiled=True)  54 us
    psum x1, blocking collectives, body(): squares = lax.psum(jnp.sum(values * values, axis=1), 'chan')  52.2 us
    ppermute x8, waiting for transfers between devices, passed_along(): return lax.ppermute(x, axis, pairs)  32.3 us
    gather x2, local copies, waits for them, and re-layouts, body(): response[jnp.clip(offsets, 0, block - 1)]  19.7 us
    ppermute x8, starting transfers between devices, passed_along(): return lax.ppermute(x, axis, pairs)  18.1 us
    dot_general x1, matrix products, body(): jnp.einsum('bsc,rscm->brcm', drive_blocks, reverse, precision=HIGHEST)  17 us
    unnamed x30, local copies, waits for them, and re-layouts  9.79 us
  transfers between devices with their start and end apart: 10, of which 8 were waited for; matrix products, arithmetic and copies ran while one was open for 15% of the time, Pallas kernels for 0%

commit v1 on v0

v1 whole, which is shorter than its diff:
```python
import jax
import jax.numpy as jnp
from jax import lax
from jax.experimental import pallas as pl
from jax.experimental.pallas import tpu as pltpu
from jax.sharding import PartitionSpec as P

MESH = pl.DeviceIdType.MESH
EPSILON = 1e-06
F32 = jnp.float32
BF16 = jnp.bfloat16

Z = 8
ROWS = 128
FEATS = 256
CH = 128
MODES = 16
SEQ = 8
MESSAGES = 41


class Place:
    def __init__(self):
        self.seq = lax.axis_index("seq")
        chan = lax.axis_index("chan")
        self.chan = chan
        self.z = chan // 4
        self.y = (chan // 2) % 2
        self.k = chan % 2

    def at(self, z, y, k):
        return (self.seq, z * 4 + y * 2 + k)

    def along(self, by):
        return (self.z + by + Z) % Z


class Gather:
    def __init__(self, place, buf, own, send_sem, recv_sem):
        self.p, self.buf, self.own = place, buf, own
        self.send_sem, self.recv_sem = send_sem, recv_sem
        p = place
        self.other_y = 1 - p.y
        self.up = p.at(p.along(1), p.y, p.k)
        self.down = p.at(p.along(-1), p.y, p.k)
        self.across = p.at(p.z, 1 - p.y, p.k)
        self.core = p.at(p.z, p.y, 1 - p.k)
        self.sent = []

    def slot(self, z, y, k, rows):
        return self.buf.at[z, y, k, pl.ds(rows[0], rows[1])]

    def copy(self, src, dst, message, device):
        return pltpu.make_async_remote_copy(
            src_ref=src,
            dst_ref=dst,
            send_sem=self.send_sem.at[message],
            recv_sem=self.recv_sem.at[message],
            device_id=device,
            device_id_type=MESH,
        )

    def send(self, z, y, rows, message, device, src=None):
        here = self.slot(z, y, self.p.k, rows)
        c = self.copy(here if src is None else src.at[pl.ds(rows[0], rows[1])], here, message, device)
        c.start()
        self.sent.append(c)

    def take(self, z, y, k, rows, message):
        here = self.slot(z, y, k, rows)
        self.copy(here, here, message, self.core).wait_recv()

    def open(self):
        p, own = self.p, self.own
        self.send(p.z, p.y, (0, 64), 0, self.across, own)
        self.send(p.z, p.y, (0, 128), 2, self.up, own)
        self.send(p.z, p.y, (0, 128), 6, self.down, own)
        self.send(p.z, p.y, (64, 64), 1, self.across, own)
        self.send(p.z, p.y, (0, 128), 25, self.core, own)

    def first(self):
        p = self.p
        self.take(p.z, self.other_y, p.k, (0, 64), 0)
        self.send(p.z, self.other_y, (0, 64), 10, self.up)
        self.send(p.z, self.other_y, (0, 64), 14, self.down)
        self.take(p.z, self.other_y, p.k, (64, 64), 1)
        self.send(p.z, self.other_y, (0, 128), 26, self.core)

    def step(self, s):
        p = self.p
        ways = ((0, p.along(-s), self.up), (1, p.along(s), self.down))
        for d, z, onward in ways:
            self.take(z, p.y, p.k, (0, 128), 2 + d * 4 + s - 1)
            rows = (0, 128) if s < 3 else (64 * d, 64)
            self.send(z, p.y, rows, 2 + d * 4 + s, onward)
            self.send(z, p.y, (64, 64), 18 + d * 3 + s - 1, self.across)
            self.send(z, p.y, (0, 128), 27 + d * 3 + s - 1, self.core)
        for d, z, onward in ways:
            self.take(z, self.other_y, p.k, (0, 64), 10 + d * 4 + s - 1)
            rows = (0, 64) if s < 3 else (32 * d, 32)
            self.send(z, self.other_y, rows, 10 + d * 4 + s, onward)
        for d, z, onward in ways:
            self.take(z, self.other_y, p.k, (64, 64), 18 + d * 3 + s - 1)
            self.send(z, self.other_y, (0, 128), 34 + d * 3 + s - 1, self.core)

    def last(self):
        p = self.p
        z = p.along(4)
        self.take(z, p.y, p.k, (0, 64), 5)
        self.take(z, p.y, p.k, (64, 64), 9)
        self.send(z, p.y, (64, 64), 24, self.across)
        self.send(z, p.y, (0, 128), 33, self.core)
        self.take(z, self.other_y, p.k, (0, 32), 13)
        self.take(z, self.other_y, p.k, (32, 32), 17)
        self.take(z, self.other_y, p.k, (64, 64), 24)
        self.send(z, self.other_y, (0, 128), 40, self.core)

    def from_core(self, s, d):
        p = self.p
        z = p.along(-s if d == 0 else s)
        if s == 0:
            first, second = 25, 26
        elif s == 4:
            first, second = 33, 40
        else:
            first, second = 27 + d * 3 + s - 1, 34 + d * 3 + s - 1
        self.take(z, p.y, 1 - p.k, (0, 128), first)
        self.take(z, self.other_y, 1 - p.k, (0, 128), second)
        return z

    def close(self):
        for c in self.sent:
            c.wait_send()


def kernel(
    tokens,
    gain,
    in_weight,
    short_filter,
    prior_rows,
    decay_rate,
    pole_angle,
    residue,
    prior_state,
    skip_weight,
    out_weight,
    mixed,
    own,
    wide,
    stats,
    weight,
    narrow,
    gated,
    last_weight,
    power_re,
    power_im,
    lift_re,
    lift_im,
    response,
    total,
    edge,
    rim,
    ext,
    padded,
    ends,
    incoming,
    local_sem,
    send1,
    recv1,
    send2,
    recv2,
    small_send,
    small_recv,
):
    p = Place()
    loads = [pltpu.make_async_copy(tokens, own, local_sem.at[0])]
    for i in range(3):
        loads.append(
            pltpu.make_async_copy(in_weight.at[i], weight.at[:, pl.ds(i * CH, CH)], local_sem.at[1 + i])
        )
    loads.append(pltpu.make_async_copy(out_weight, last_weight, local_sem.at[4]))
    for c in loads:
        c.start()

    barrier = pltpu.get_barrier_semaphore()
    greeted = [p.at(p.z, p.y, 1 - p.k), p.at(p.z, 1 - p.y, p.k), p.at(p.z, 1 - p.y, 1 - p.k)]
    greeted += [p.at(p.along(i), p.y, p.k) for i in range(1, Z)]
    greeted += [((p.seq + i) % SEQ, p.chan) for i in range(1, SEQ)]
    for device in greeted:
        pl.semaphore_signal(barrier, inc=1, device_id=device, device_id_type=MESH)

    loads[0].wait()
    values = own[...].astype(F32)
    squares = jnp.sum(values * values, axis=1, keepdims=True)
    row = jnp.broadcast_to(squares, (ROWS, 128)).T
    gains = gain[...].astype(F32)
    stats[p.z, 2 * p.y + p.k] = jnp.concatenate(
        [row[0:1], gains[:, 0:128], gains[:, 128:256], row[3:8]], axis=0
    )
    wide[p.z, p.y, p.k] = own[...]

    pl.semaphore_wait(barrier, len(greeted))

    def small(src, dst, index, device):
        return pltpu.make_async_remote_copy(
            src_ref=src,
            dst_ref=dst,
            send_sem=small_send.at[index],
            recv_sem=small_recv.at[index],
            device_id=device,
            device_id_type=MESH,
        )

    small_sent = []
    mine = stats.at[p.z, 2 * p.y + p.k]
    for i, (dy, dk) in enumerate(((0, 1), (1, 0), (1, 1))):
        y = (p.y + dy) % 2
        k = (p.k + dk) % 2
        c = small(mine, mine, i, p.at(p.z, y, k))
        c.start()
        small_sent.append(c)
    spread = Gather(p, wide, own, send1, recv1)
    spread.open()
    for i, (dy, dk) in enumerate(((0, 1), (1, 0), (1, 1))):
        y = (p.y + dy) % 2
        k = (p.k + dk) % 2
        theirs = stats.at[p.z, 2 * y + k]
        small(theirs, theirs, i, p.at(p.z, y, k)).wait_recv()
    for i in range(1, Z):
        c = small(stats.at[p.z], stats.at[p.z], 2 + i, p.at(p.along(i), p.y, p.k))
        c.start()
        small_sent.append(c)
    spread.first()
    spread.step(1)

    magnitude = jnp.exp(-decay_rate[...])
    pole_re = magnitude * jnp.cos(pole_angle[...])
    pole_im = magnitude * jnp.sin(pole_angle[...])
    res_re = residue[0]
    res_im = residue[1]

    def tabulate(t, carry):
        re, im, lre, lim = carry
        power_re[t] = re
        power_im[t] = im
        response[pl.ds(t, 1)] = jnp.sum(lre, axis=0, keepdims=True)
        lre, lim = pole_re * lre - pole_im * lim, pole_re * lim + pole_im * lre
        lift_re[t] = lre
        lift_im[t] = lim
        return (pole_re * re - pole_im * im, pole_re * im + pole_im * re, lre, lim)

    one = jnp.ones((MODES, CH), F32)
    shard_re, shard_im, _, _ = lax.fori_loop(
        0, ROWS, tabulate, (one, jnp.zeros_like(one), res_re, res_im)
    )
    padded[pl.ds(0, ROWS)] = jnp.zeros((ROWS, CH), F32)
    total[...] = jnp.zeros_like(total)

    for i in range(1, Z):
        z = p.along(-i)
        small(stats.at[z], stats.at[z], 2 + i, p.at(z, p.y, p.k)).wait_recv()
    summed = jnp.zeros((1, 128), F32)
    for z in range(Z):
        for j in range(4):
            summed = summed + stats[z, j, 0:1]
    scale_row = lax.rsqrt(summed / (FEATS * 4 * Z) + EPSILON)
    scale = jnp.broadcast_to(scale_row, (ROWS, 128)).T

    def project(z):
        parts = []
        for j in range(4):
            x = wide[z, j // 2, j % 2].astype(F32)
            for h in range(2):
                part = x[:, 128 * h : 128 * h + 128] * scale * stats[z, j, 1 + h : 2 + h]
                parts.append(part.astype(BF16))
        normed = jnp.concatenate(parts, axis=1)
        rows = weight[pl.ds(pl.multiple_of(z * 4 * FEATS, 4 * FEATS), 4 * FEATS)]
        total[...] += jnp.dot(normed, rows, preferred_element_type=F32)

    for c in loads[1:4]:
        c.wait()
    spread.step(2)
    project(spread.from_core(0, 0))
    project(spread.from_core(1, 0))
    spread.step(3)
    project(spread.from_core(1, 1))
    project(spread.from_core(2, 0))
    spread.last()
    project(spread.from_core(2, 1))
    project(spread.from_core(3, 0))
    project(spread.from_core(3, 1))
    project(spread.from_core(4, 0))

    projected = total[...].astype(BF16)
    edge[...] = projected[ROWS - 16 :]
    after = ((p.seq + 1) % SEQ, p.chan)
    halo = small(edge, rim, 10, after)

    @pl.when(p.seq < SEQ - 1)
    def _():
        halo.start()

    ext[pl.ds(16, ROWS)] = projected.astype(F32)

    @pl.when(p.seq == 0)
    def _():
        for i in range(3):
            ext[pl.ds(14, 2), pl.ds(i * CH, CH)] = prior_rows[i].astype(F32)

    @pl.when(p.seq > 0)
    def _():
        halo.wait_recv()
        ext[pl.ds(0, 16)] = rim[...].astype(F32)

    convolved = []
    for i in range(3):
        lanes = pl.ds(i * CH, CH)
        c = jnp.zeros((ROWS, CH), F32)
        for lag in range(3):
            c = c + short_filter[lag, i : i + 1] * ext[pl.ds(16 - lag, ROWS), lanes]
        convolved.append(c)
    query = convolved[0]
    drive = convolved[1] * convolved[2]
    padded[pl.ds(ROWS, ROWS)] = drive

    def gather_end(i, carry):
        out = []
        for j in range(4):
            re, im = carry[j]
            t = 4 * i + j
            u = padded[pl.ds(ROWS + t, 1)]
            out.append((re + power_re[ROWS - 1 - t] * u, im + power_im[ROWS - 1 - t] * u))
        return tuple(out)

    nothing = jnp.zeros((MODES, CH), F32)
    sums = lax.fori_loop(0, ROWS // 4, gather_end, ((nothing, nothing),) * 4)
    ends[p.seq, 0] = sums[0][0] + sums[1][0] + sums[2][0] + sums[3][0]
    ends[p.seq, 1] = sums[0][1] + sums[1][1] + sums[2][1] + sums[3][1]
    here = ends.at[p.seq]
    for i in range(1, SEQ):

        @pl.when(p.seq + i < SEQ)
        def _():
            small(here, here, 10 + i, ((p.seq + i) % SEQ, p.chan)).start()

    def respond(i, acc):
        for j in range(4):
            lag = 4 * i + j
            acc = acc + response[pl.ds(lag, 1)] * padded[pl.ds(ROWS - lag, ROWS)]
        return acc

    mode_out = lax.fori_loop(0, ROWS // 4, respond, jnp.zeros((ROWS, CH), F32))

    incoming[...] = prior_state[...]
    for j in range(SEQ - 1):

        @pl.when(j < p.seq)
        def _():
            theirs = ends.at[j]
            for i in range(1, SEQ):

                @pl.when(p.seq - j == i)
                def _():
                    small(theirs, theirs, 10 + i, (j, p.chan)).wait_recv()

            re, im = incoming[0], incoming[1]
            incoming[0] = shard_re * re - shard_im * im + ends[j, 0]
            incoming[1] = shard_re * im + shard_im * re + ends[j, 1]

    in_re, in_im = incoming[0], incoming[1]
    carried = []
    for b in range(ROWS // 8):
        lre = lift_re[pl.ds(8 * b, 8)]
        lim = lift_im[pl.ds(8 * b, 8)]
        carried.append(jnp.sum(lre * in_re[None] - lim * in_im[None], axis=1))
    mode_out = mode_out + jnp.concatenate(carried, axis=0)
    gated[...] = (query * (mode_out + skip_weight[...] * drive)).astype(BF16)
    narrow[p.z, p.y, p.k] = gated[...]

    mix = Gather(p, narrow, gated, send2, recv2)
    mix.open()
    loads[4].wait()

    def output(z):
        parts = [narrow[z, j // 2, j % 2] for j in range(4)]
        rows = last_weight[pl.ds(pl.multiple_of(z * 4 * CH, 4 * CH), 4 * CH)]
        return jnp.dot(jnp.concatenate(parts, axis=1), rows, preferred_element_type=F32)

    mix.first()
    mix.step(1)
    acc = output(mix.from_core(0, 0))
    mix.step(2)
    acc = acc + output(mix.from_core(1, 0))
    acc = acc + output(mix.from_core(1, 1))
    mix.step(3)
    acc = acc + output(mix.from_core(2, 0))
    acc = acc + output(mix.from_core(2, 1))
    mix.last()
    acc = acc + output(mix.from_core(3, 0))
    acc = acc + output(mix.from_core(3, 1))
    acc = acc + output(mix.from_core(4, 0))
    mixed[...] = (own[...].astype(F32) + acc).astype(BF16)

    for c in small_sent:
        c.wait_send()
    spread.close()
    mix.close()

    @pl.when(p.seq < SEQ - 1)
    def _():
        halo.wait_send()

    for i in range(1, SEQ):

        @pl.when(p.seq + i < SEQ)
        def _():
            small(here, here, 10 + i, ((p.seq + i) % SEQ, p.chan)).wait_send()


def body(
    tokens,
    norm_gain,
    in_weight,
    short_filter,
    prior_rows,
    decay_rate,
    pole_angle,
    residue,
    prior_state,
    skip_weight,
    out_weight,
):
    vmem = pl.BlockSpec(memory_space=pltpu.VMEM)
    hbm = pl.BlockSpec(memory_space=pl.ANY)
    flops = 2 * ROWS * (FEATS * 32 * 3 * CH + CH * 32 * FEATS)
    return pl.pallas_call(
        kernel,
        out_shape=jax.ShapeDtypeStruct((ROWS, FEATS), BF16),
        in_specs=[hbm, vmem, hbm, vmem, vmem, vmem, vmem, vmem, vmem, vmem, hbm],
        out_specs=vmem,
        scratch_shapes=[
            pltpu.VMEM((ROWS, FEATS), BF16),
            pltpu.VMEM((Z, 2, 2, ROWS, FEATS), BF16),
            pltpu.VMEM((Z, 4, 8, 128), F32),
            pltpu.VMEM((Z * 4 * FEATS, 3 * CH), BF16),
            pltpu.VMEM((Z, 2, 2, ROWS, CH), BF16),
            pltpu.VMEM((ROWS, CH), BF16),
            pltpu.VMEM((Z * 4 * CH, FEATS), BF16),
            pltpu.VMEM((ROWS, MODES, CH), F32),
            pltpu.VMEM((ROWS, MODES, CH), F32),
            pltpu.VMEM((ROWS, MODES, CH), F32),
            pltpu.VMEM((ROWS, MODES, CH), F32),
            pltpu.VMEM((ROWS, CH), F32),
            pltpu.VMEM((ROWS, 3 * CH), F32),
            pltpu.VMEM((16, 3 * CH), BF16),
            pltpu.VMEM((16, 3 * CH), BF16),
            pltpu.VMEM((16 + ROWS, 3 * CH), F32),
            pltpu.VMEM((2 * ROWS, CH), F32),
            pltpu.VMEM((SEQ, 2, MODES, CH), F32),
            pltpu.VMEM((2, MODES, CH), F32),
            pltpu.SemaphoreType.DMA((5,)),
            pltpu.SemaphoreType.DMA((MESSAGES,)),
            pltpu.SemaphoreType.DMA((MESSAGES,)),
            pltpu.SemaphoreType.DMA((MESSAGES,)),
            pltpu.SemaphoreType.DMA((MESSAGES,)),
            pltpu.SemaphoreType.DMA((18,)),
            pltpu.SemaphoreType.DMA((18,)),
        ],
        compiler_params=pltpu.CompilerParams(
            collective_id=0, has_side_effects=True, vmem_limit_bytes=40 * 1024 * 1024
        ),
        cost_estimate=pl.CostEstimate(flops=flops, bytes_accessed=9 * 1024 * 1024, transcendentals=0),
    )(
        tokens,
        norm_gain.reshape(1, FEATS),
        jnp.transpose(in_weight, (1, 0, 2)),
        short_filter,
        jnp.transpose(prior_rows, (1, 0, 2)),
        decay_rate.T,
        pole_angle.T,
        jnp.transpose(residue, (0, 2, 1)),
        jnp.transpose(prior_state, (0, 2, 1)),
        skip_weight.reshape(1, CH),
        out_weight,
    )


def solution(mesh):
    return jax.shard_map(
        body,
        mesh=mesh,
        in_specs=(
            P("seq", "chan"),
            P("chan"),
            P(None, None, "chan"),
            P(None, None, "chan"),
            P(None, None, "chan"),
            P("chan", None),
            P("chan", None),
            P(None, "chan", None),
            P(None, "chan", None),
            P("chan"),
            P(None, "chan"),
        ),
        out_specs=P("seq", "chan"),
        check_vma=False,
    )
```

time: 342 us -> 72.7 us (0.21)
  waiting for transfers between devices: 155 us -> 0 us
  Pallas kernels: 0 us -> 60.9 us
  blocking collectives: 52.2 us -> 0 us
  matrix products: 35.3 us -> 0 us
  local copies, waits for them, and re-layouts: 44.3 us -> 11.4 us
  other arithmetic: 20.8 us -> 0 us
  starting transfers between devices: 18.1 us -> 0 us
  between operations: 13.8 us -> 0.02 us
    all_gather x2 -> x0, waiting for transfers between devices: 123 us -> none  [the longest x1 68.5 us: body(): lax.all_gather(gated, 'chan', axis=1, tiled=True)]
    pallas_call x0 -> x1, Pallas kernels: none -> 60.9 us  [body(): pl.pallas_call(kernel, out_shape=jax.ShapeDtypeStruct((ROWS, FEATS), BF16...]
    psum x1 -> x0, blocking collectives: 52.2 us -> none  [body(): squares = lax.psum(jnp.sum(values * values, axis=1), 'chan')]
    dot_general x6 -> x0, matrix products: 35.3 us -> none  [the longest x1 17 us: body(): jnp.einsum('bsc,rscm->brcm', drive_blocks, reverse, precision=HIGHEST)]
    ppermute x8 -> x0, waiting for transfers between devices: 32.3 us -> none  [passed_along(): return lax.ppermute(x, axis, pairs)]
    gather x2 -> x0, local copies, waits for them, and re-layouts: 19.7 us -> none  [body(): response[jnp.clip(offsets, 0, block - 1)]]
    ppermute x8 -> x0, starting transfers between devices: 18.1 us -> none  [passed_along(): return lax.ppermute(x, axis, pairs)]
    rev x2 -> x0, local copies, waits for them, and re-layouts: 6.39 us -> none  [body(): reverse = table[:, :block][:, ::-1]]
  transfers between devices with their start and end apart: 10 -> 0, of which waited for: 8 -> 0; matrix products, arithmetic and copies ran while one was open for 15% -> 0% of each run, Pallas kernels for 0% -> 0%
where the time goes in v1:
time: 72.7 us; the launch traced here: 72.2 us
  Pallas kernels  60.9 us (84%)
  local copies, waits for them, and re-layouts  11.4 us (16%)
    pallas_call x1, Pallas kernels, body(): pl.pallas_call(kernel, out_shape=jax.ShapeDtypeStruct((ROWS, FEATS), BF16...  60.9 us
    unnamed x21, local copies, waits for them, and re-layouts  10.7 us

profile of v1, /device:TPU:25, one launch (start us, length us, event | category | flops | bytes accessed | tf_op | source)
XLA Modules:
  0.0 72.2 jit_solution(10313034797766228026)
XLA Ops:
  0.0 0.7 reshape.6.gain
  0.7 0.0 copy-start
  0.7 2.8 %copy-done = bf16[8192,3,128]{2,0,1:T(8,128)(2,1)S(1)} copy-done((bf16[8192,3,128]{2,0,1:T(8,128)(2,1)S(1)}, bf16[8192,3,128]{2,0,1:T(8,128)(2,1)}, u32[]{:S(2)}) %copy-start) | copy-done | bytes 6291480
  3.4 0.0 copy-start.1
  3.4 1.6 %copy-done.1 = bf16[4096,256]{1,0:T(8,128)(2,1)S(1)} copy-done((bf16[4096,256]{1,0:T(8,128)(2,1)S(1)}, bf16[4096,256]{1,0:T(8,128)(2,1)}, u32[]{:S(2)}) %copy-start.1) | copy-done | bytes 2097176
  5.0 0.0 copy-start.2
  5.0 0.8 %copy-done.2 = bf16[128,256]{1,0:T(8,128)(2,1)S(1)} copy-done((bf16[128,256]{1,0:T(8,128)(2,1)S(1)}, bf16[128,256]{1,0:T(8,128)(2,1)}, u32[]{:S(2)}) %copy-start.2) | copy-done | bytes 65560
  5.9 0.0 copy-start.3
  5.9 0.7 copy-done.3
  6.6 0.0 copy-start.4
  6.6 0.7 copy-done.4
  7.3 0.0 copy-start.5
  7.3 0.7 copy-done.5
  8.0 0.0 copy-start.6
  8.0 0.7 copy-done.6
  8.7 0.0 copy-start.7
  8.7 0.7 copy-done.7
  9.4 0.0 copy-start.8
  9.4 0.7 copy-done.8
  10.1 0.0 copy-start.9
  10.1 0.7 copy-done.9
  10.7 60.9 %shard_map.109 = bf16[128,256]{1,0:T(8,128)(2,1)S(1)} custom-call(bf16[128,256]{1,0:T(8,128)(2,1)S(1)} %copy-done.2, bf16[1,256]{1,0:T(2,128)(2,1)S(1)} %reshape.6.gain, bf16[3,8192,128]{2,1,0:T(8,128)(2,1)S(1)} %bitcast.7, f32[3,3,128]{2,1,0:T(4,128)S(1)} %copy-done.7, bf16[3,2,128]{2,1,0:T(2,128)(2,1)S(1)} %bitcast.12, f32[16,128]{1,0:T(8,128)S(1)} %bitcast.10, ...), custom_call_target="tpu_custom_call" | custom-call | flops 1073741824 | bytes 9437184 | tf_op jit(solution)/shard_map/pallas_call | solution.py:437
  71.6 0.6 copy.13
Async XLA Ops:
  0.7 2.8 %copy-start = (bf16[8192,3,128]{2,0,1:T(8,128)(2,1)S(1)}, bf16[8192,3,128]{2,0,1:T(8,128)(2,1)}, u32[]{:S(2)}) copy-start(bf16[8192,3,128]{2,0,1:T(8,128)(2,1)} %param.13) | copy-start | bytes 18874372
  3.4 1.6 %copy-start.1 = (bf16[4096,256]{1,0:T(8,128)(2,1)S(1)}, bf16[4096,256]{1,0:T(8,128)(2,1)}, u32[]{:S(2)}) copy-start(bf16[4096,256]{1,0:T(8,128)(2,1)} %out_weight.1) | copy-start | bytes 6291460
  5.0 0.8 %copy-start.2 = (bf16[128,256]{1,0:T(8,128)(2,1)S(1)}, bf16[128,256]{1,0:T(8,128)(2,1)}, u32[]{:S(2)}) copy-start(bf16[128,256]{1,0:T(8,128)(2,1)} %tokens.1) | copy-start | bytes 196612
  5.9 0.7 copy-start.3
  6.6 0.7 copy-start.4
  7.3 0.7 copy-start.5
  8.0 0.7 copy-start.6
  8.7 0.7 copy-start.7
  9.4 0.7 copy-start.8
  10.1 0.7 copy-start.9

commit v2 on v1

v2 whole, which is shorter than its diff:
```python
import jax
import jax.numpy as jnp
from jax import lax
from jax.experimental import pallas as pl
from jax.experimental.pallas import tpu as pltpu
from jax.sharding import PartitionSpec as P

MESH = pl.DeviceIdType.MESH
EPSILON = 1e-06
F32 = jnp.float32
BF16 = jnp.bfloat16

Z = 8
ROWS = 128
FEATS = 256
CH = 128
MODES = 16
SEQ = 8


class Place:
    def __init__(self):
        self.seq = lax.axis_index("seq")
        chan = lax.axis_index("chan")
        self.chan = chan
        self.z = chan // 4
        self.y = (chan // 2) % 2
        self.k = chan % 2

    def at(self, z, y, k):
        return (self.seq, z * 4 + y * 2 + k)

    def to(self, dz, dy, dk):
        return self.at(self.along(dz), (self.y + dy) % 2, (self.k + dk) % 2)

    def along(self, by):
        return (self.z + by + Z) % Z


WIDE_PLAN = (
    (0, 0, 0, 128, 2, 0, 0),
    (0, 0, 0, 128, -2, 0, 0),
    (0, 0, 0, 128, 1, 0, 0),
    (0, 0, 0, 128, -1, 0, 0),
    (0, 0, 0, 128, 0, 1, 0),
    (0, 0, 0, 128, 0, 0, 1),
    "tables",
    "stats2",
    (0, 1, 64, 64, 2, 0, 0),
    (0, 1, 64, 64, -2, 0, 0),
    (0, 1, 0, 128, 0, 0, 1),
    (-2, 0, 32, 32, 2, 0, 0),
    (2, 0, 0, 32, -2, 0, 0),
    (-2, 0, 96, 32, 2, 0, 0),
    (-2, 0, 0, 96, 1, 0, 0),
    (2, 0, 0, 96, -1, 0, 0),
    (-2, 0, 0, 64, 0, 1, 0),
    (2, 0, 0, 64, 0, 1, 0),
    (-2, 0, 0, 128, 0, 0, 1),
    (2, 0, 0, 128, 0, 0, 1),
    "stats3",
    (-1, 0, 96, 32, 2, 0, 0),
    (1, 0, 64, 32, -3, 0, 0),
    (1, 0, 96, 32, -2, 0, 0),
    (-1, 0, 0, 128, 0, 1, 0),
    (1, 0, 0, 128, 0, 1, 0),
    (-1, 0, 0, 128, 0, 0, 1),
    (1, 0, 0, 128, 0, 0, 1),
    (-2, 1, 96, 32, 2, 0, 0),
    (2, 1, 64, 32, -2, 0, 0),
    (-2, 1, 0, 128, 1, 0, 0),
    (-2, 1, 0, 128, 0, 0, 1),
    (4, 0, 0, 64, 0, 1, 0),
    (2, 1, 32, 96, -1, 0, 0),
    (2, 1, 0, 128, 0, 0, 1),
    "scale",
    (3, 0, 0, 32, 0, 1, 0),
    0,
    -2,
    (-1, 1, 0, 128, 0, 0, 1),
    2,
    (-3, 0, 0, 128, 0, 0, 1),
    (4, 0, 0, 128, 0, 0, 1),
    (3, 0, 0, 128, 0, 0, 1),
    (1, 1, 0, 128, 0, 0, 1),
    -1,
    (4, 1, 0, 128, 0, 0, 1),
    (-3, 1, 0, 128, 0, 0, 1),
    (3, 1, 0, 128, 0, 0, 1),
    1,
    4,
    -3,
    3,
)

NARROW_PLAN = (
    (0, 0, 0, 128, 3, 0, 0),
    (0, 0, 0, 128, -3, 0, 0),
    (0, 0, 0, 128, 2, 0, 0),
    (0, 0, 0, 128, -2, 0, 0),
    (0, 0, 0, 128, 1, 0, 0),
    (0, 0, 0, 128, -1, 0, 0),
    (0, 0, 0, 128, 0, 1, 0),
    (0, 0, 0, 128, 0, 0, 1),
    (0, 1, 0, 128, 4, 0, 0),
    (0, 1, 0, 128, -2, 0, 0),
    (0, 1, 0, 128, 1, 0, 0),
    (0, 1, 0, 128, -1, 0, 0),
    (0, 1, 0, 128, 0, 0, 1),
    0,
    (-3, 0, 0, 128, 0, 1, 0),
    (3, 0, 0, 128, -1, 0, 0),
    (3, 0, 0, 128, 0, 1, 0),
    (-3, 0, 0, 128, 0, 0, 1),
    (3, 0, 0, 128, 0, 0, 1),
    (-2, 0, 0, 128, 0, 1, 0),
    (-2, 0, 0, 128, 0, 0, 1),
    (2, 0, 0, 128, 0, 0, 1),
    (-1, 0, 0, 128, 0, 0, 1),
    (1, 0, 0, 128, 0, 0, 1),
    (2, 1, 0, 128, 0, 0, 1),
    (-3, 1, 0, 128, 0, 0, 1),
    (1, 1, 0, 128, 0, 0, 1),
    (3, 1, 0, 128, 0, 0, 1),
    (4, 0, 0, 128, 0, 0, 1),
    2,
    (-1, 1, 0, 128, 0, 0, 1),
    (-2, 1, 0, 128, 0, 0, 1),
    -3,
    1,
    (4, 1, 0, 128, 0, 0, 1),
    3,
    -1,
    -2,
    4,
)


def nearest(dz):
    dz %= Z
    return dz - Z if dz > Z // 2 else dz


class Gather:
    def __init__(self, place, buf, plan, send_sem, recv_sem):
        self.p, self.buf, self.plan = place, buf, plan
        self.send_sem, self.recv_sem = send_sem, recv_sem
        self.sends = [step for step in plan if isinstance(step, tuple)]
        self.brings = {}
        for i, (dz, dy, first, rows, tz, ty, tk) in enumerate(self.sends):
            for r in range(first, first + rows, 16):
                self.brings[nearest(dz - tz), dy ^ ty, tk, r] = i
        self.waited = set()
        self.sent = []

    def copy(self, i, block, device):
        p = self.p
        dz, dy, dk = block
        first, rows = self.sends[i][2:4]
        here = self.buf.at[p.along(dz), (p.y + dy) % 2, (p.k + dk) % 2, pl.ds(first, rows)]
        return pltpu.make_async_remote_copy(
            src_ref=here,
            dst_ref=here,
            send_sem=self.send_sem.at[i],
            recv_sem=self.recv_sem.at[i],
            device_id=device,
            device_id_type=MESH,
        )

    def need(self, block, first, rows):
        if block == (0, 0, 0):
            return
        for r in range(first, first + rows, 16):
            i = self.brings[block + (r,)]
            if i not in self.waited:
                self.waited.add(i)
                dz, dy, _, _, tz, ty, tk = self.sends[i]
                self.copy(i, (nearest(dz - tz), dy ^ ty, tk), self.p.to(0, 0, 1)).wait_recv()

    def run(self, on_chip, named):
        for step in self.plan:
            if isinstance(step, str):
                named[step]()
            elif isinstance(step, int):
                for block in ((step, 0, 0), (step, 1, 0), (step, 0, 1), (step, 1, 1)):
                    self.need(block, 0, ROWS)
                on_chip(self.p.along(step))
            else:
                dz, dy, first, rows, tz, ty, tk = step
                self.need((nearest(dz), dy, 0), first, rows)
                c = self.copy(len(self.sent), (dz, dy, 0), self.p.to(tz, ty, tk))
                c.start()
                self.sent.append(c)

    def close(self):
        for c in self.sent:
            c.wait_send()


def kernel(
    tokens,
    gain_hbm,
    in_weight,
    filter_hbm,
    rows_hbm,
    decay_hbm,
    angle_hbm,
    residue_hbm,
    state_hbm,
    skip_hbm,
    out_weight,
    mixed,
    gain,
    short_filter,
    prior_rows,
    decay_rate,
    pole_angle,
    residue,
    skip_weight,
    own,
    wide,
    stats,
    weight,
    narrow,
    last_weight,
    power_re,
    power_im,
    lift_re,
    lift_im,
    response,
    total,
    edge,
    rim,
    ext,
    padded,
    ends,
    incoming,
    shard_power,
    scales,
    hello,
    local_sem,
    send1,
    recv1,
    send2,
    recv2,
    small_send,
    small_recv,
):
    p = Place()
    pairs = (
        (tokens, own),
        (gain_hbm, gain),
        (filter_hbm, short_filter),
        (rows_hbm, prior_rows),
        (decay_hbm, decay_rate),
        (angle_hbm, pole_angle),
        (residue_hbm, residue),
        (state_hbm, incoming),
        (skip_hbm, skip_weight),
    )
    loads = [pltpu.make_async_copy(a, b, local_sem.at[4 + i]) for i, (a, b) in enumerate(pairs)]
    weight_loads = []
    for i in range(3):
        weight_loads.append(
            pltpu.make_async_copy(in_weight.at[i], weight.at[:, pl.ds(i * CH, CH)], local_sem.at[i])
        )
    last_load = pltpu.make_async_copy(out_weight, last_weight, local_sem.at[3])
    for c in loads + weight_loads + [last_load]:
        c.start()

    barrier = pltpu.get_barrier_semaphore()
    kin = [
        (4 * (p.seq // 4) + (p.seq + 1) % 4, p.chan),
        (4 * (p.seq // 4) + (p.seq + 3) % 4, p.chan),
        ((p.seq + 4) % SEQ, p.chan),
    ]
    greeted = [p.to(*by) for by in ((0, 0, 1), (0, 1, 0), (0, 1, 1), (1, 0, 0), (-1, 0, 0), (2, 0, 0), (-2, 0, 0))]
    greeted += kin
    for device in greeted:
        pl.semaphore_signal(barrier, inc=1, device_id=device, device_id_type=MESH)

    loads[0].wait()
    loads[1].wait()
    values = own[...].astype(F32)
    squares = jnp.sum(values * values, axis=1, keepdims=True)
    row = jnp.broadcast_to(squares, (ROWS, 128)).T
    gains = gain[...].astype(F32).reshape(1, FEATS)
    stats[p.z, 2 * p.y + p.k] = jnp.concatenate(
        [row[0:1], gains[:, 0:128], gains[:, 128:256], row[3:8]], axis=0
    )
    wide[p.z, p.y, p.k] = own[...]

    pl.semaphore_wait(barrier, len(greeted))

    def small(src, dst, index, device):
        return pltpu.make_async_remote_copy(
            src_ref=src,
            dst_ref=dst,
            send_sem=small_send.at[index],
            recv_sem=small_recv.at[index],
            device_id=device,
            device_id_type=MESH,
        )

    small_sent = []

    def spread_small(src, index, device):
        c = small(src, src, index, device)
        c.start()
        small_sent.append(c)

    def small_here(z, index):
        small(stats.at[z], stats.at[z], index, p.to(0, 0, 1)).wait_recv()

    pair = ((0, 1), (1, 0), (1, 1))
    for i, (dy, dk) in enumerate(pair):
        spread_small(stats.at[p.z, 2 * p.y + p.k], i, p.to(0, dy, dk))
    for device in kin:
        pl.semaphore_signal(hello.at[0], inc=1, device_id=device, device_id_type=MESH)

    def stats2():
        for i, (dy, dk) in enumerate(pair):
            theirs = stats.at[p.z, 2 * ((p.y + dy) % 2) + (p.k + dk) % 2]
            small(theirs, theirs, i, p.to(0, dy, dk)).wait_recv()
        for i, by in enumerate((1, -1, 2, -2)):
            spread_small(stats.at[p.z], 3 + i, p.to(by, 0, 0))
        pl.semaphore_wait(hello.at[0], len(kin))
        for device in kin:
            pl.semaphore_signal(hello.at[1], inc=1, device_id=device, device_id_type=MESH)

    def stats3():
        small_here(p.along(-2), 5)
        small_here(p.along(2), 6)
        spread_small(stats.at[p.along(-2)], 7, p.to(1, 0, 0))
        spread_small(stats.at[p.along(2)], 8, p.to(-1, 0, 0))
        spread_small(stats.at[p.along(-2)], 9, p.to(2, 0, 0))

    def tables():
        for c in loads[2:]:
            c.wait()
        magnitude = jnp.exp(-decay_rate[...])
        pole_re = magnitude * jnp.cos(pole_angle[...])
        pole_im = magnitude * jnp.sin(pole_angle[...])
        res_re = residue[0]
        res_im = residue[1]

        def tabulate(t, carry):
            re, im, lre, lim = carry
            power_re[t] = re
            power_im[t] = im
            response[pl.ds(t, 1)] = jnp.sum(lre, axis=0, keepdims=True)
            lre, lim = pole_re * lre - pole_im * lim, pole_re * lim + pole_im * lre
            lift_re[t] = lre
            lift_im[t] = lim
            return (pole_re * re - pole_im * im, pole_re * im + pole_im * re, lre, lim)

        one = jnp.ones((MODES, CH), F32)
        end_re, end_im, _, _ = lax.fori_loop(
            0, ROWS, tabulate, (one, jnp.zeros_like(one), res_re, res_im)
        )
        padded[pl.ds(0, ROWS)] = jnp.zeros((ROWS, CH), F32)
        total[...] = jnp.zeros_like(total)
        shard_power[0] = end_re
        shard_power[1] = end_im

    def find_scale():
        small_here(p.along(-1), 3)
        small_here(p.along(1), 4)
        small_here(p.along(-3), 7)
        small_here(p.along(3), 8)
        small_here(p.along(4), 9)
        pl.semaphore_wait(hello.at[1], len(kin))
        summed = jnp.zeros((1, 128), F32)
        for z in range(Z):
            for j in range(4):
                summed = summed + stats[z, j, 0:1]
        scale_row = lax.rsqrt(summed / (FEATS * 4 * Z) + EPSILON)
        scales[...] = jnp.broadcast_to(scale_row, (ROWS, 128)).T
        for c in weight_loads:
            c.wait()

    def project(z):
        parts = []
        scale = scales[...]
        for j in range(4):
            x = wide[z, j // 2, j % 2].astype(F32)
            for h in range(2):
                part = x[:, 128 * h : 128 * h + 128] * scale * stats[z, j, 1 + h : 2 + h]
                parts.append(part.astype(BF16))
        normed = jnp.concatenate(parts, axis=1)
        rows = weight[pl.ds(pl.multiple_of(z * 4 * FEATS, 4 * FEATS), 4 * FEATS)]
        total[...] += jnp.dot(normed, rows, preferred_element_type=F32)

    spread = Gather(p, wide, WIDE_PLAN, send1, recv1)
    spread.run(project, {"tables": tables, "stats2": stats2, "stats3": stats3, "scale": find_scale})

    def close_spread():
        for c in small_sent:
            c.wait_send()
        spread.close()

    projected = total[...].astype(BF16)
    edge[...] = projected[ROWS - 16 :]
    after = ((p.seq + 1) % SEQ, p.chan)
    halo = small(edge, rim, 10, after)

    @pl.when(p.seq < SEQ - 1)
    def _():
        halo.start()

    ext[pl.ds(16, ROWS)] = projected.astype(F32)

    @pl.when(p.seq == 0)
    def _():
        for i in range(3):
            ext[pl.ds(14, 2), pl.ds(i * CH, CH)] = prior_rows[i].astype(F32)

    @pl.when(p.seq > 0)
    def _():
        halo.wait_recv()
        ext[pl.ds(0, 16)] = rim[...].astype(F32)

    def close_halo():
        @pl.when(p.seq < SEQ - 1)
        def _():
            halo.wait_send()

    convolved = []
    for i in range(3):
        lanes = pl.ds(i * CH, CH)
        c = jnp.zeros((ROWS, CH), F32)
        for lag in range(3):
            c = c + short_filter[lag, i : i + 1] * ext[pl.ds(16 - lag, ROWS), lanes]
        convolved.append(c)
    query = convolved[0]
    drive = convolved[1] * convolved[2]
    padded[pl.ds(ROWS, ROWS)] = drive

    def gather_end(i, carry):
        out = []
        for j in range(4):
            re, im = carry[j]
            t = 4 * i + j
            u = padded[pl.ds(ROWS + t, 1)]
            out.append((re + power_re[ROWS - 1 - t] * u, im + power_im[ROWS - 1 - t] * u))
        return tuple(out)

    nothing = jnp.zeros((MODES, CH), F32)
    sums = lax.fori_loop(0, ROWS // 4, gather_end, ((nothing, nothing),) * 4)
    ends[p.seq, 0] = sums[0][0] + sums[1][0] + sums[2][0] + sums[3][0]
    ends[p.seq, 1] = sums[0][1] + sums[1][1] + sums[2][1] + sums[3][1]
    here = ends.at[p.seq]
    for i in range(1, SEQ):

        @pl.when(p.seq + i < SEQ)
        def _():
            small(here, here, 10 + i, ((p.seq + i) % SEQ, p.chan)).start()

    def close_state():
        for i in range(1, SEQ):

            @pl.when(p.seq + i < SEQ)
            def _():
                small(here, here, 10 + i, ((p.seq + i) % SEQ, p.chan)).wait_send()

    def respond(i, acc):
        for j in range(4):
            lag = 4 * i + j
            acc = acc + response[pl.ds(lag, 1)] * padded[pl.ds(ROWS - lag, ROWS)]
        return acc

    mode_out = lax.fori_loop(0, ROWS // 4, respond, jnp.zeros((ROWS, CH), F32))

    shard_re, shard_im = shard_power[0], shard_power[1]
    for j in range(SEQ - 1):

        @pl.when(j < p.seq)
        def _():
            theirs = ends.at[j]
            for i in range(1, SEQ):

                @pl.when(p.seq - j == i)
                def _():
                    small(theirs, theirs, 10 + i, (j, p.chan)).wait_recv()

            re, im = incoming[0], incoming[1]
            incoming[0] = shard_re * re - shard_im * im + ends[j, 0]
            incoming[1] = shard_re * im + shard_im * re + ends[j, 1]

    in_re, in_im = incoming[0], incoming[1]
    carried = []
    for b in range(ROWS // 8):
        lre = lift_re[pl.ds(8 * b, 8)]
        lim = lift_im[pl.ds(8 * b, 8)]
        carried.append(jnp.sum(lre * in_re[None] - lim * in_im[None], axis=1))
    mode_out = mode_out + jnp.concatenate(carried, axis=0)
    narrow[p.z, p.y, p.k] = (query * (mode_out + skip_weight[...] * drive)).astype(BF16)

    total[:, pl.ds(0, FEATS)] = own[...].astype(F32)
    last_load.wait()

    def output(z):
        parts = [narrow[z, j // 2, j % 2] for j in range(4)]
        rows = last_weight[pl.ds(pl.multiple_of(z * 4 * CH, 4 * CH), 4 * CH)]
        total[:, pl.ds(0, FEATS)] += jnp.dot(
            jnp.concatenate(parts, axis=1), rows, preferred_element_type=F32
        )

    mix = Gather(p, narrow, NARROW_PLAN, send2, recv2)
    mix.run(output, {})
    mixed[...] = total[:, pl.ds(0, FEATS)].astype(BF16)

    mix.close()
    close_state()
    close_halo()
    close_spread()


def body(
    tokens,
    norm_gain,
    in_weight,
    short_filter,
    prior_rows,
    decay_rate,
    pole_angle,
    residue,
    prior_state,
    skip_weight,
    out_weight,
):
    vmem = pl.BlockSpec(memory_space=pltpu.VMEM)
    hbm = pl.BlockSpec(memory_space=pltpu.HBM)
    flops = 2 * ROWS * (FEATS * 32 * 3 * CH + CH * 32 * FEATS)
    return pl.pallas_call(
        kernel,
        out_shape=jax.ShapeDtypeStruct((ROWS, FEATS), BF16),
        in_specs=[hbm] * 11,
        out_specs=vmem,
        scratch_shapes=[
            pltpu.VMEM((FEATS,), BF16),
            pltpu.VMEM((3, 3, CH), F32),
            pltpu.VMEM((3, 2, CH), BF16),
            pltpu.VMEM((MODES, CH), F32),
            pltpu.VMEM((MODES, CH), F32),
            pltpu.VMEM((2, MODES, CH), F32),
            pltpu.VMEM((1, CH), F32),
            pltpu.VMEM((ROWS, FEATS), BF16),
            pltpu.VMEM((Z, 2, 2, ROWS, FEATS), BF16),
            pltpu.VMEM((Z, 4, 8, 128), F32),
            pltpu.VMEM((Z * 4 * FEATS, 3 * CH), BF16),
            pltpu.VMEM((Z, 2, 2, ROWS, CH), BF16),
            pltpu.VMEM((Z * 4 * CH, FEATS), BF16),
            pltpu.VMEM((ROWS, MODES, CH), F32),
            pltpu.VMEM((ROWS, MODES, CH), F32),
            pltpu.VMEM((ROWS, MODES, CH), F32),
            pltpu.VMEM((ROWS, MODES, CH), F32),
            pltpu.VMEM((ROWS, CH), F32),
            pltpu.VMEM((ROWS, 3 * CH), F32),
            pltpu.VMEM((16, 3 * CH), BF16),
            pltpu.VMEM((16, 3 * CH), BF16),
            pltpu.VMEM((16 + ROWS, 3 * CH), F32),
            pltpu.VMEM((2 * ROWS, CH), F32),
            pltpu.VMEM((SEQ, 2, MODES, CH), F32),
            pltpu.VMEM((2, MODES, CH), F32),
            pltpu.VMEM((2, MODES, CH), F32),
            pltpu.VMEM((ROWS, 128), F32),
            pltpu.SemaphoreType.REGULAR((2,)),
            pltpu.SemaphoreType.DMA((13,)),
            pltpu.SemaphoreType.DMA((len(WIDE_PLAN),)),
            pltpu.SemaphoreType.DMA((len(WIDE_PLAN),)),
            pltpu.SemaphoreType.DMA((len(NARROW_PLAN),)),
            pltpu.SemaphoreType.DMA((len(NARROW_PLAN),)),
            pltpu.SemaphoreType.DMA((18,)),
            pltpu.SemaphoreType.DMA((18,)),
        ],
        compiler_params=pltpu.CompilerParams(
            collective_id=0, has_side_effects=True, vmem_limit_bytes=60 * 1024 * 1024
        ),
        cost_estimate=pl.CostEstimate(flops=flops, bytes_accessed=9 * 1024 * 1024, transcendentals=0),
    )(
        tokens,
        norm_gain,
        jnp.transpose(in_weight, (1, 0, 2)),
        short_filter,
        jnp.transpose(prior_rows, (1, 0, 2)),
        decay_rate.T,
        pole_angle.T,
        jnp.transpose(residue, (0, 2, 1)),
        jnp.transpose(prior_state, (0, 2, 1)),
        skip_weight.reshape(1, CH),
        out_weight,
    )


def solution(mesh):
    return jax.shard_map(
        body,
        mesh=mesh,
        in_specs=(
            P("seq", "chan"),
            P("chan"),
            P(None, None, "chan"),
            P(None, None, "chan"),
            P(None, None, "chan"),
            P("chan", None),
            P("chan", None),
            P(None, "chan", None),
            P(None, "chan", None),
            P("chan"),
            P(None, "chan"),
        ),
        out_specs=P("seq", "chan"),
        check_vma=False,
    )
```

time: 72.7 us -> 48.4 us (0.67)
  Pallas kernels: 60.9 us -> 46.8 us
  local copies, waits for them, and re-layouts: 11.4 us -> 1.47 us
    pallas_call x1, Pallas kernels: 60.9 us -> 46.8 us  [body(): pl.pallas_call(kernel, out_shape=jax.ShapeDtypeStruct((ROWS, FEATS), BF16...]
    unnamed x21 -> x1, local copies, waits for them, and re-layouts: 10.7 us -> 1.47 us
where the time goes in v2:
time: 48.4 us; the launch traced here: 48.2 us
  Pallas kernels  46.8 us (97%)
  local copies, waits for them, and re-layouts  1.47 us (3%)
    pallas_call x1, Pallas kernels, body(): pl.pallas_call(kernel, out_shape=jax.ShapeDtypeStruct((ROWS, FEATS), BF16...  46.8 us
    unnamed x1, local copies, waits for them, and re-layouts  1.47 us

profile of v2, /device:TPU:25, one launch (start us, length us, event | category | flops | bytes accessed | tf_op | source)
XLA Modules:
  0.0 48.2 jit_solution(15207774069972657103)
XLA Ops:
  0.0 46.8 %shard_map.109 = bf16[128,256]{1,0:T(8,128)(2,1)} custom-call(bf16[128,256]{1,0:T(8,128)(2,1)} %tokens.1, bf16[256]{0:T(256)(128)(2,1)} %gain_hbm.1, bf16[3,8192,128]{2,1,0:T(8,128)(2,1)} %bitcast.7, f32[3,3,128]{2,1,0:T(4,128)} %filter_hbm.1, bf16[3,2,128]{2,1,0:T(2,128)(2,1)} %bitcast.12, f32[16,128]{1,0:T(8,128)} %bitcast.10, f32[16,128]{1,0:T(8,128)} %bitcast.11, ...), custom_call_target="tpu_custom_call" | custom-call | flops 1073741824 | bytes 9437184 | tf_op jit(solution)/shard_map/pallas_call | solution.py:535
  46.8 1.5 %copy.13 = bf16[128,256]{1,0:T(8,128)(2,1)} copy(bf16[128,256]{1,0:T(8,128)(2,1)} %shard_map.109) | data formatting | bytes 131072

commit v3 on v2

--- a/solution.py
+++ b/solution.py
@@ -44,6 +44,7 @@
     (0, 0, 0, 128, -1, 0, 0),
     (0, 0, 0, 128, 0, 1, 0),
     (0, 0, 0, 128, 0, 0, 1),
+    "stats1",
     "tables",
     "stats2",
     (0, 1, 64, 64, 2, 0, 0),
@@ -118,12 +119,14 @@
     (2, 0, 0, 128, 0, 0, 1),
     (-1, 0, 0, 128, 0, 0, 1),
     (1, 0, 0, 128, 0, 0, 1),
+    "settle",
     (2, 1, 0, 128, 0, 0, 1),
     (-3, 1, 0, 128, 0, 0, 1),
     (1, 1, 0, 128, 0, 0, 1),
     (3, 1, 0, 128, 0, 0, 1),
     (4, 0, 0, 128, 0, 0, 1),
     2,
+    "settle",
     (-1, 1, 0, 128, 0, 0, 1),
     (-2, 1, 0, 128, 0, 0, 1),
     -3,
@@ -142,8 +145,8 @@
 
 
 class Gather:
-    def __init__(self, place, buf, plan, send_sem, recv_sem):
-        self.p, self.buf, self.plan = place, buf, plan
+    def __init__(self, place, buf, own, plan, send_sem, recv_sem):
+        self.p, self.buf, self.own, self.plan = place, buf, own, plan
         self.send_sem, self.recv_sem = send_sem, recv_sem
         self.sends = [step for step in plan if isinstance(step, tuple)]
         self.brings = {}
@@ -152,14 +155,16 @@
                 self.brings[nearest(dz - tz), dy ^ ty, tk, r] = i
         self.waited = set()
         self.sent = []
+        self.settled = 0
 
     def copy(self, i, block, device):
         p = self.p
         dz, dy, dk = block
         first, rows = self.sends[i][2:4]
         here = self.buf.at[p.along(dz), (p.y + dy) % 2, (p.k + dk) % 2, pl.ds(first, rows)]
+        mine = self.own is not None and block == (0, 0, 0)
         return pltpu.make_async_remote_copy(
-            src_ref=here,
+            src_ref=self.own.at[pl.ds(first, rows)] if mine else here,
             dst_ref=here,
             send_sem=self.send_sem.at[i],
             recv_sem=self.recv_sem.at[i],
@@ -192,9 +197,11 @@
                 c.start()
                 self.sent.append(c)
 
-    def close(self):
-        for c in self.sent:
+    def settle(self, in_flight=0):
+        upto = max(self.settled, len(self.sent) - in_flight)
+        for c in self.sent[self.settled : upto]:
             c.wait_send()
+        self.settled = upto
 
 
 def kernel(
@@ -229,7 +236,6 @@
     lift_im,
     response,
     total,
-    edge,
     rim,
     ext,
     padded,
@@ -247,6 +253,17 @@
     small_recv,
 ):
     p = Place()
+    barrier = pltpu.get_barrier_semaphore()
+    kin = [
+        (4 * (p.seq // 4) + (p.seq + 1) % 4, p.chan),
+        (4 * (p.seq // 4) + (p.seq + 3) % 4, p.chan),
+        ((p.seq + 4) % SEQ, p.chan),
+    ]
+    greeted = [p.to(*by) for by in ((0, 0, 1), (0, 1, 0), (0, 1, 1), (1, 0, 0), (-1, 0, 0), (2, 0, 0), (-2, 0, 0))]
+    greeted += kin
+    for device in greeted:
+        pl.semaphore_signal(barrier, inc=1, device_id=device, device_id_type=MESH)
+
     pairs = (
         (tokens, own),
         (gain_hbm, gain),
@@ -268,28 +285,6 @@
     for c in loads + weight_loads + [last_load]:
         c.start()
 
-    barrier = pltpu.get_barrier_semaphore()
-    kin = [
-        (4 * (p.seq // 4) + (p.seq + 1) % 4, p.chan),
-        (4 * (p.seq // 4) + (p.seq + 3) % 4, p.chan),
-        ((p.seq + 4) % SEQ, p.chan),
-    ]
-    greeted = [p.to(*by) for by in ((0, 0, 1), (0, 1, 0), (0, 1, 1), (1, 0, 0), (-1, 0, 0), (2, 0, 0), (-2, 0, 0))]
-    greeted += kin
-    for device in greeted:
-        pl.semaphore_signal(barrier, inc=1, device_id=device, device_id_type=MESH)
-
-    loads[0].wait()
-    loads[1].wait()
-    values = own[...].astype(F32)
-    squares = jnp.sum(values * values, axis=1, keepdims=True)
-    row = jnp.broadcast_to(squares, (ROWS, 128)).T
-    gains = gain[...].astype(F32).reshape(1, FEATS)
-    stats[p.z, 2 * p.y + p.k] = jnp.concatenate(
-        [row[0:1], gains[:, 0:128], gains[:, 128:256], row[3:8]], axis=0
-    )
-    wide[p.z, p.y, p.k] = own[...]
-
     pl.semaphore_wait(barrier, len(greeted))
 
     def small(src, dst, index, device):
@@ -313,10 +308,22 @@
         small(stats.at[z], stats.at[z], index, p.to(0, 0, 1)).wait_recv()
 
     pair = ((0, 1), (1, 0), (1, 1))
-    for i, (dy, dk) in enumerate(pair):
-        spread_small(stats.at[p.z, 2 * p.y + p.k], i, p.to(0, dy, dk))
-    for device in kin:
-        pl.semaphore_signal(hello.at[0], inc=1, device_id=device, device_id_type=MESH)
+
+    def stats1():
+        loads[0].wait()
+        loads[1].wait()
+        values = own[...].astype(F32)
+        squares = jnp.sum(values * values, axis=1, keepdims=True)
+        row = jnp.broadcast_to(squares, (ROWS, 128)).T
+        gains = gain[...].astype(F32).reshape(1, FEATS)
+        stats[p.z, 2 * p.y + p.k] = jnp.concatenate(
+            [row[0:1], gains[:, 0:128], gains[:, 128:256], row[3:8]], axis=0
+        )
+        wide[p.z, p.y, p.k] = own[...]
+        for i, (dy, dk) in enumerate(pair):
+            spread_small(stats.at[p.z, 2 * p.y + p.k], i, p.to(0, dy, dk))
+        for device in kin:
+            pl.semaphore_signal(hello.at[0], inc=1, device_id=device, device_id_type=MESH)
 
     def stats2():
         for i, (dy, dk) in enumerate(pair):
@@ -348,7 +355,7 @@
             re, im, lre, lim = carry
             power_re[t] = re
             power_im[t] = im
-            response[pl.ds(t, 1)] = jnp.sum(lre, axis=0, keepdims=True)
+            response[pl.ds(8 + t, 1)] = jnp.sum(lre, axis=0, keepdims=True)
             lre, lim = pole_re * lre - pole_im * lim, pole_re * lim + pole_im * lre
             lift_re[t] = lre
             lift_im[t] = lim
@@ -359,6 +366,7 @@
             0, ROWS, tabulate, (one, jnp.zeros_like(one), res_re, res_im)
         )
         padded[pl.ds(0, ROWS)] = jnp.zeros((ROWS, CH), F32)
+        response[pl.ds(0, 8)] = jnp.zeros((8, CH), F32)
         total[...] = jnp.zeros_like(total)
         shard_power[0] = end_re
         shard_power[1] = end_im
@@ -391,49 +399,30 @@
         rows = weight[pl.ds(pl.multiple_of(z * 4 * FEATS, 4 * FEATS), 4 * FEATS)]
         total[...] += jnp.dot(normed, rows, preferred_element_type=F32)
 
-    spread = Gather(p, wide, WIDE_PLAN, send1, recv1)
-    spread.run(project, {"tables": tables, "stats2": stats2, "stats3": stats3, "scale": find_scale})
+    spread = Gather(p, wide, tokens, WIDE_PLAN, send1, recv1)
+    spread.run(
+        project,
+        {"stats1": stats1, "tables": tables, "stats2": stats2, "stats3": stats3, "scale": find_scale},
+    )
 
     def close_spread():
         for c in small_sent:
             c.wait_send()
-        spread.close()
-
-    projected = total[...].astype(BF16)
-    edge[...] = projected[ROWS - 16 :]
-    after = ((p.seq + 1) % SEQ, p.chan)
-    halo = small(edge, rim, 10, after)
-
-    @pl.when(p.seq < SEQ - 1)
-    def _():
-        halo.start()
-
-    ext[pl.ds(16, ROWS)] = projected.astype(F32)
-
-    @pl.when(p.seq == 0)
-    def _():
-        for i in range(3):
-            ext[pl.ds(14, 2), pl.ds(i * CH, CH)] = prior_rows[i].astype(F32)
-
-    @pl.when(p.seq > 0)
-    def _():
-        halo.wait_recv()
-        ext[pl.ds(0, 16)] = rim[...].astype(F32)
-
-    def close_halo():
-        @pl.when(p.seq < SEQ - 1)
-        def _():
-            halo.wait_send()
-
+        spread.settle()
+
+    projected = total[...].astype(BF16).astype(F32)
+    ext[pl.ds(0, 8)] = jnp.zeros((8, 3 * CH), F32)
+    ext[pl.ds(8, ROWS)] = projected
     convolved = []
     for i in range(3):
         lanes = pl.ds(i * CH, CH)
         c = jnp.zeros((ROWS, CH), F32)
         for lag in range(3):
-            c = c + short_filter[lag, i : i + 1] * ext[pl.ds(16 - lag, ROWS), lanes]
+            c = c + short_filter[lag, i : i + 1] * ext[pl.ds(8 - lag, ROWS), lanes]
         convolved.append(c)
-    query = convolved[0]
-    drive = convolved[1] * convolved[2]
+    query, key, value = convolved
+    row_of = lax.broadcasted_iota(jnp.int32, (ROWS, CH), 0)
+    drive = jnp.where(row_of < 2, 0.0, key * value)
     padded[pl.ds(ROWS, ROWS)] = drive
 
     def gather_end(i, carry):
@@ -447,31 +436,56 @@
 
     nothing = jnp.zeros((MODES, CH), F32)
     sums = lax.fori_loop(0, ROWS // 4, gather_end, ((nothing, nothing),) * 4)
-    ends[p.seq, 0] = sums[0][0] + sums[1][0] + sums[2][0] + sums[3][0]
-    ends[p.seq, 1] = sums[0][1] + sums[1][1] + sums[2][1] + sums[3][1]
+
+    edges = [projected[ROWS - 2 :, i * CH : i * CH + CH] for i in range(3)]
+    edges += [jnp.zeros((2, CH), F32), key[0:2], value[0:2], jnp.zeros((4, CH), F32)]
+    ends[p.seq, pl.ds(0, MODES)] = sums[0][0] + sums[1][0] + sums[2][0] + sums[3][0]
+    ends[p.seq, pl.ds(MODES, MODES)] = sums[0][1] + sums[1][1] + sums[2][1] + sums[3][1]
+    ends[p.seq, pl.ds(2 * MODES, 16)] = jnp.concatenate(edges, axis=0)
     here = ends.at[p.seq]
-    for i in range(1, SEQ):
+
+    def end_copy(i):
+        return small(here, here, 10 + i, ((p.seq + i) % SEQ, p.chan))
+
+    for i in (6, 5, 7, 4, 2, 3, 1):
 
         @pl.when(p.seq + i < SEQ)
         def _():
-            small(here, here, 10 + i, ((p.seq + i) % SEQ, p.chan)).start()
+            end_copy(i).start()
 
     def close_state():
         for i in range(1, SEQ):
 
             @pl.when(p.seq + i < SEQ)
             def _():
-                small(here, here, 10 + i, ((p.seq + i) % SEQ, p.chan)).wait_send()
+                end_copy(i).wait_send()
 
     def respond(i, acc):
         for j in range(4):
             lag = 4 * i + j
-            acc = acc + response[pl.ds(lag, 1)] * padded[pl.ds(ROWS - lag, ROWS)]
+            acc = acc + response[pl.ds(8 + lag, 1)] * padded[pl.ds(ROWS - lag, ROWS)]
         return acc
 
     mode_out = lax.fori_loop(0, ROWS // 4, respond, jnp.zeros((ROWS, CH), F32))
-
+    close_spread()
+
+    def first_rows(i, so_far):
+        near, far = short_filter[1, i : i + 1], short_filter[2, i : i + 1]
+        before = rim[pl.ds(2 * i, 2)]
+        return (
+            so_far[0:1] + near * before[1:2] + far * before[0:1],
+            so_far[1:2] + far * before[1:2],
+        )
+
+    def first_drive(key_rows, value_rows):
+        (key0, key1), (value0, value1) = first_rows(1, key_rows), first_rows(2, value_rows)
+        return key0 * value0, key1 * value1
+
+    for i in range(3):
+        rim[pl.ds(2 * i, 2)] = prior_rows[i].astype(F32)
     shard_re, shard_im = shard_power[0], shard_power[1]
+    last_re, last_im = power_re[ROWS - 1], power_im[ROWS - 1]
+    next_re, next_im = power_re[ROWS - 2], power_im[ROWS - 2]
     for j in range(SEQ - 1):
 
         @pl.when(j < p.seq)
@@ -483,9 +497,13 @@
                 def _():
                     small(theirs, theirs, 10 + i, (j, p.chan)).wait_recv()
 
+            drive0, drive1 = first_drive(ends[j, pl.ds(40, 2)], ends[j, pl.ds(42, 2)])
             re, im = incoming[0], incoming[1]
-            incoming[0] = shard_re * re - shard_im * im + ends[j, 0]
-            incoming[1] = shard_re * im + shard_im * re + ends[j, 1]
+            end_re = ends[j, pl.ds(0, MODES)] + last_re * drive0 + next_re * drive1
+            end_im = ends[j, pl.ds(MODES, MODES)] + last_im * drive0 + next_im * drive1
+            incoming[0] = shard_re * re - shard_im * im + end_re
+            incoming[1] = shard_re * im + shard_im * re + end_im
+            rim[pl.ds(0, 6)] = ends[j, pl.ds(32, 6)]
 
     in_re, in_im = incoming[0], incoming[1]
     carried = []
@@ -493,6 +511,12 @@
         lre = lift_re[pl.ds(8 * b, 8)]
         lim = lift_im[pl.ds(8 * b, 8)]
         carried.append(jnp.sum(lre * in_re[None] - lim * in_im[None], axis=1))
+    drive0, drive1 = first_drive(key[0:2], value[0:2])
+    query0, query1 = first_rows(0, query[0:2])
+    first, second = row_of == 0, row_of == 1
+    drive = jnp.where(first, drive0, jnp.where(second, drive1, drive))
+    query = jnp.where(first, query0, jnp.where(second, query1, query))
+    mode_out = mode_out + response[pl.ds(8, ROWS)] * drive0 + response[pl.ds(7, ROWS)] * drive1
     mode_out = mode_out + jnp.concatenate(carried, axis=0)
     narrow[p.z, p.y, p.k] = (query * (mode_out + skip_weight[...] * drive)).astype(BF16)
 
@@ -506,14 +530,17 @@
             jnp.concatenate(parts, axis=1), rows, preferred_element_type=F32
         )
 
-    mix = Gather(p, narrow, NARROW_PLAN, send2, recv2)
-    mix.run(output, {})
+    mix = Gather(p, narrow, None, NARROW_PLAN, send2, recv2)
+
+    def settle():
+        if not mix.settled:
+            close_state()
+        mix.settle(in_flight=8)
+
+    mix.run(output, {"settle": settle})
     mixed[...] = total[:, pl.ds(0, FEATS)].astype(BF16)
 
-    mix.close()
-    close_state()
-    close_halo()
-    close_spread()
+    mix.settle()
 
 
 def body(
@@ -555,13 +582,12 @@
             pltpu.VMEM((ROWS, MODES, CH), F32),
             pltpu.VMEM((ROWS, MODES, CH), F32),
             pltpu.VMEM((ROWS, MODES, CH), F32),
-            pltpu.VMEM((ROWS, CH), F32),
+            pltpu.VMEM((8 + ROWS, CH), F32),
             pltpu.VMEM((ROWS, 3 * CH), F32),
-            pltpu.VMEM((16, 3 * CH), BF16),
-            pltpu.VMEM((16, 3 * CH), BF16),
-            pltpu.VMEM((16 + ROWS, 3 * CH), F32),
+            pltpu.VMEM((8, CH), F32),
+            pltpu.VMEM((8 + ROWS, 3 * CH), F32),
             pltpu.VMEM((2 * ROWS, CH), F32),
-            pltpu.VMEM((SEQ, 2, MODES, CH), F32),
+            pltpu.VMEM((SEQ, 2 * MODES + 16, CH), F32),
             pltpu.VMEM((2, MODES, CH), F32),
             pltpu.VMEM((2, MODES, CH), F32),
             pltpu.VMEM((ROWS, 128), F32),

time: 48.4 us -> 46.8 us (0.967)
  Pallas kernels: 46.8 us -> 45.2 us
    pallas_call x1, Pallas kernels: 46.8 us -> 45.2 us  [body(): pl.pallas_call(kernel, out_shape=jax.ShapeDtypeStruct((ROWS, FEATS), BF16...]
where the time goes in v3:
time: 46.8 us; the launch traced here: 46.7 us
  Pallas kernels  45.2 us (97%)
  local copies, waits for them, and re-layouts  1.47 us (3%)
    pallas_call x1, Pallas kernels, body(): pl.pallas_call(kernel, out_shape=jax.ShapeDtypeStruct((ROWS, FEATS), BF16...  45.2 us
    unnamed x1, local copies, waits for them, and re-layouts  1.47 us

profile of v3, /device:TPU:25, one launch (start us, length us, event | category | flops | bytes accessed | tf_op | source)
XLA Modules:
  0.0 46.7 jit_solution(3414152686175016900)
XLA Ops:
  0.0 45.2 %shard_map.109 = bf16[128,256]{1,0:T(8,128)(2,1)} custom-call(bf16[128,256]{1,0:T(8,128)(2,1)} %tokens.1, bf16[256]{0:T(256)(128)(2,1)} %gain_hbm.1, bf16[3,8192,128]{2,1,0:T(8,128)(2,1)} %bitcast.7, f32[3,3,128]{2,1,0:T(4,128)} %filter_hbm.1, bf16[3,2,128]{2,1,0:T(2,128)(2,1)} %bitcast.12, f32[16,128]{1,0:T(8,128)} %bitcast.10, f32[16,128]{1,0:T(8,128)} %bitcast.11, ...), custom_call_target="tpu_custom_call" | custom-call | flops 1073741824 | bytes 9437184 | tf_op jit(solution)/shard_map/pallas_call | solution.py:562
  45.2 1.5 %copy.13 = bf16[128,256]{1,0:T(8,128)(2,1)} copy(bf16[128,256]{1,0:T(8,128)(2,1)} %shard_map.109) | data formatting | bytes 131072

commit v4 on v3

--- a/solution.py
+++ b/solution.py
@@ -46,7 +46,6 @@
     (0, 0, 0, 128, 0, 0, 1),
     "stats1",
     "tables",
-    "stats2",
     (0, 1, 64, 64, 2, 0, 0),
     (0, 1, 64, 64, -2, 0, 0),
     (0, 1, 0, 128, 0, 0, 1),
@@ -59,11 +58,12 @@
     (2, 0, 0, 64, 0, 1, 0),
     (-2, 0, 0, 128, 0, 0, 1),
     (2, 0, 0, 128, 0, 0, 1),
-    "stats3",
     (-1, 0, 96, 32, 2, 0, 0),
     (1, 0, 64, 32, -3, 0, 0),
     (1, 0, 96, 32, -2, 0, 0),
     (-1, 0, 0, 128, 0, 1, 0),
+    "stats2",
+    "stats3",
     (1, 0, 0, 128, 0, 1, 0),
     (-1, 0, 0, 128, 0, 0, 1),
     (1, 0, 0, 128, 0, 0, 1),
@@ -74,20 +74,20 @@
     (4, 0, 0, 64, 0, 1, 0),
     (2, 1, 32, 96, -1, 0, 0),
     (2, 1, 0, 128, 0, 0, 1),
-    "scale",
     (3, 0, 0, 32, 0, 1, 0),
-    0,
-    -2,
     (-1, 1, 0, 128, 0, 0, 1),
-    2,
     (-3, 0, 0, 128, 0, 0, 1),
     (4, 0, 0, 128, 0, 0, 1),
     (3, 0, 0, 128, 0, 0, 1),
     (1, 1, 0, 128, 0, 0, 1),
-    -1,
     (4, 1, 0, 128, 0, 0, 1),
     (-3, 1, 0, 128, 0, 0, 1),
     (3, 1, 0, 128, 0, 0, 1),
+    "scale",
+    0,
+    -2,
+    2,
+    -1,
     1,
     4,
     -3,
@@ -317,7 +317,7 @@
         row = jnp.broadcast_to(squares, (ROWS, 128)).T
         gains = gain[...].astype(F32).reshape(1, FEATS)
         stats[p.z, 2 * p.y + p.k] = jnp.concatenate(
-            [row[0:1], gains[:, 0:128], gains[:, 128:256], row[3:8]], axis=0
+            [row[0:1], gains[:, 0:128], gains[:, 128:256], row[3:4]], axis=0
         )
         wide[p.z, p.y, p.k] = own[...]
         for i, (dy, dk) in enumerate(pair):
@@ -331,16 +331,10 @@
             small(theirs, theirs, i, p.to(0, dy, dk)).wait_recv()
         for i, by in enumerate((1, -1, 2, -2)):
             spread_small(stats.at[p.z], 3 + i, p.to(by, 0, 0))
-        pl.semaphore_wait(hello.at[0], len(kin))
-        for device in kin:
-            pl.semaphore_signal(hello.at[1], inc=1, device_id=device, device_id_type=MESH)
 
     def stats3():
-        small_here(p.along(-2), 5)
-        small_here(p.along(2), 6)
-        spread_small(stats.at[p.along(-2)], 7, p.to(1, 0, 0))
-        spread_small(stats.at[p.along(2)], 8, p.to(-1, 0, 0))
-        spread_small(stats.at[p.along(-2)], 9, p.to(2, 0, 0))
+        for i, by in enumerate((3, -3, 4)):
+            spread_small(stats.at[p.z], 7 + i, p.to(by, 0, 0))
 
     def tables():
         for c in loads[2:]:
@@ -372,12 +366,11 @@
         shard_power[1] = end_im
 
     def find_scale():
-        small_here(p.along(-1), 3)
-        small_here(p.along(1), 4)
-        small_here(p.along(-3), 7)
-        small_here(p.along(3), 8)
-        small_here(p.along(4), 9)
-        pl.semaphore_wait(hello.at[1], len(kin))
+        for i, by in enumerate((1, -1, 2, -2, 3, -3, 4)):
+            small_here(p.along(-by), 3 + i)
+        pl.semaphore_wait(hello.at[0], len(kin))
+        for device in kin:
+            pl.semaphore_signal(hello.at[1], inc=1, device_id=device, device_id_type=MESH)
         summed = jnp.zeros((1, 128), F32)
         for z in range(Z):
             for j in range(4):
@@ -447,6 +440,7 @@
     def end_copy(i):
         return small(here, here, 10 + i, ((p.seq + i) % SEQ, p.chan))
 
+    pl.semaphore_wait(hello.at[1], len(kin))
     for i in (6, 5, 7, 4, 2, 3, 1):
 
         @pl.when(p.seq + i < SEQ)
@@ -574,7 +568,7 @@
             pltpu.VMEM((1, CH), F32),
             pltpu.VMEM((ROWS, FEATS), BF16),
             pltpu.VMEM((Z, 2, 2, ROWS, FEATS), BF16),
-            pltpu.VMEM((Z, 4, 8, 128), F32),
+            pltpu.VMEM((Z, 4, 4, 128), F32),
             pltpu.VMEM((Z * 4 * FEATS, 3 * CH), BF16),
             pltpu.VMEM((Z, 2, 2, ROWS, CH), BF16),
             pltpu.VMEM((Z * 4 * CH, FEATS), BF16),

time: 46.8 us -> 45.6 us (0.974)
  Pallas kernels: 45.2 us -> 44 us
    pallas_call x1, Pallas kernels: 45.2 us -> 44 us  [body(): pl.pallas_call(kernel, out_shape=jax.ShapeDtypeStruct((ROWS, FEATS), BF16...]
where the time goes in v4:
time: 45.6 us; the launch traced here: 45.5 us
  Pallas kernels  44 us (96%)
  local copies, waits for them, and re-layouts  1.47 us (3%)
    pallas_call x1, Pallas kernels, body(): pl.pallas_call(kernel, out_shape=jax.ShapeDtypeStruct((ROWS, FEATS), BF16...  44 us
    unnamed x1, local copies, waits for them, and re-layouts  1.47 us

profile of v4, /device:TPU:25, one launch (start us, length us, event | category | flops | bytes accessed | tf_op | source)
XLA Modules:
  0.0 45.5 jit_solution(14382011270888203989)
XLA Ops:
  0.0 44.0 %shard_map.109 = bf16[128,256]{1,0:T(8,128)(2,1)} custom-call(bf16[128,256]{1,0:T(8,128)(2,1)} %tokens.1, bf16[256]{0:T(256)(128)(2,1)} %gain_hbm.1, bf16[3,8192,128]{2,1,0:T(8,128)(2,1)} %bitcast.7, f32[3,3,128]{2,1,0:T(4,128)} %filter_hbm.1, bf16[3,2,128]{2,1,0:T(2,128)(2,1)} %bitcast.12, f32[16,128]{1,0:T(8,128)} %bitcast.10, f32[16,128]{1,0:T(8,128)} %bitcast.11, ...), custom_call_target="tpu_custom_call" | custom-call | flops 1073741824 | bytes 9437184 | tf_op jit(solution)/shard_map/pallas_call | solution.py:556
  44.1 1.5 %copy.13 = bf16[128,256]{1,0:T(8,128)(2,1)} copy(bf16[128,256]{1,0:T(8,128)(2,1)} %shard_map.109) | data formatting | bytes 131072

commit v5 on v4

--- a/solution.py
+++ b/solution.py
@@ -103,6 +103,7 @@
     (0, 0, 0, 128, -1, 0, 0),
     (0, 0, 0, 128, 0, 1, 0),
     (0, 0, 0, 128, 0, 0, 1),
+    "begin",
     (0, 1, 0, 128, 4, 0, 0),
     (0, 1, 0, 128, -2, 0, 0),
     (0, 1, 0, 128, 1, 0, 0),
@@ -406,29 +407,25 @@
     projected = total[...].astype(BF16).astype(F32)
     ext[pl.ds(0, 8)] = jnp.zeros((8, 3 * CH), F32)
     ext[pl.ds(8, ROWS)] = projected
-    convolved = []
-    for i in range(3):
+
+    def convolve(i):
         lanes = pl.ds(i * CH, CH)
         c = jnp.zeros((ROWS, CH), F32)
         for lag in range(3):
             c = c + short_filter[lag, i : i + 1] * ext[pl.ds(8 - lag, ROWS), lanes]
-        convolved.append(c)
-    query, key, value = convolved
+        return c
+
+    key, value = convolve(1), convolve(2)
     row_of = lax.broadcasted_iota(jnp.int32, (ROWS, CH), 0)
     drive = jnp.where(row_of < 2, 0.0, key * value)
     padded[pl.ds(ROWS, ROWS)] = drive
 
-    def gather_end(i, carry):
-        out = []
-        for j in range(4):
-            re, im = carry[j]
-            t = 4 * i + j
-            u = padded[pl.ds(ROWS + t, 1)]
-            out.append((re + power_re[ROWS - 1 - t] * u, im + power_im[ROWS - 1 - t] * u))
-        return tuple(out)
-
     nothing = jnp.zeros((MODES, CH), F32)
-    sums = lax.fori_loop(0, ROWS // 4, gather_end, ((nothing, nothing),) * 4)
+    sums = [[nothing, nothing] for _ in range(4)]
+    for t in range(2, ROWS):
+        u = padded[pl.ds(ROWS + t, 1)]
+        sums[t % 4][0] += power_re[ROWS - 1 - t] * u
+        sums[t % 4][1] += power_im[ROWS - 1 - t] * u
 
     edges = [projected[ROWS - 2 :, i * CH : i * CH + CH] for i in range(3)]
     edges += [jnp.zeros((2, CH), F32), key[0:2], value[0:2], jnp.zeros((4, CH), F32)]
@@ -453,6 +450,8 @@
             @pl.when(p.seq + i < SEQ)
             def _():
                 end_copy(i).wait_send()
+
+    query = convolve(0)
 
     def respond(i, acc):
         for j in range(4):
@@ -514,8 +513,9 @@
     mode_out = mode_out + jnp.concatenate(carried, axis=0)
     narrow[p.z, p.y, p.k] = (query * (mode_out + skip_weight[...] * drive)).astype(BF16)
 
-    total[:, pl.ds(0, FEATS)] = own[...].astype(F32)
-    last_load.wait()
+    def begin():
+        total[:, pl.ds(0, FEATS)] = own[...].astype(F32)
+        last_load.wait()
 
     def output(z):
         parts = [narrow[z, j // 2, j % 2] for j in range(4)]
@@ -531,7 +531,7 @@
             close_state()
         mix.settle(in_flight=8)
 
-    mix.run(output, {"settle": settle})
+    mix.run(output, {"begin": begin, "settle": settle})
     mixed[...] = total[:, pl.ds(0, FEATS)].astype(BF16)
 
     mix.settle()

time: 45.6 us -> 45.4 us (level)
  no operation moved by 1% of the time
where the time goes in v5:
time: 45.4 us; the launch traced here: 45.3 us
  Pallas kernels  43.8 us (96%)
  local copies, waits for them, and re-layouts  1.47 us (3%)
    pallas_call x1, Pallas kernels, body(): pl.pallas_call(kernel, out_shape=jax.ShapeDtypeStruct((ROWS, FEATS), BF16...  43.8 us
    unnamed x1, local copies, waits for them, and re-layouts  1.47 us

profile of v5, /device:TPU:25, one launch (start us, length us, event | category | flops | bytes accessed | tf_op | source)
XLA Modules:
  0.0 45.3 jit_solution(5244307568882267577)
XLA Ops:
  0.0 43.8 %shard_map.109 = bf16[128,256]{1,0:T(8,128)(2,1)} custom-call(bf16[128,256]{1,0:T(8,128)(2,1)} %tokens.1, bf16[256]{0:T(256)(128)(2,1)} %gain_hbm.1, bf16[3,8192,128]{2,1,0:T(8,128)(2,1)} %bitcast.7, f32[3,3,128]{2,1,0:T(4,128)} %filter_hbm.1, bf16[3,2,128]{2,1,0:T(2,128)(2,1)} %bitcast.12, f32[16,128]{1,0:T(8,128)} %bitcast.10, f32[16,128]{1,0:T(8,128)} %bitcast.11, ...), custom_call_target="tpu_custom_call" | custom-call | flops 1073741824 | bytes 9437184 | tf_op jit(solution)/shard_map/pallas_call | solution.py:556
  43.8 1.5 %copy.13 = bf16[128,256]{1,0:T(8,128)(2,1)} copy(bf16[128,256]{1,0:T(8,128)(2,1)} %shard_map.109) | data formatting | bytes 131072

commit v6 on v5

--- a/solution.py
+++ b/solution.py
@@ -95,48 +95,49 @@
 )
 
 NARROW_PLAN = (
+    (0, 0, 0, 64, 4, 1, 0),
+    (0, 0, 0, 128, -3, 0, 0),
     (0, 0, 0, 128, 3, 0, 0),
-    (0, 0, 0, 128, -3, 0, 0),
-    (0, 0, 0, 128, 2, 0, 0),
-    (0, 0, 0, 128, -2, 0, 0),
+    (0, 0, 0, 128, -1, 0, 0),
     (0, 0, 0, 128, 1, 0, 0),
-    (0, 0, 0, 128, -1, 0, 0),
     (0, 0, 0, 128, 0, 1, 0),
     (0, 0, 0, 128, 0, 0, 1),
     "begin",
-    (0, 1, 0, 128, 4, 0, 0),
+    (0, 1, 64, 64, 4, 0, 0),
     (0, 1, 0, 128, -2, 0, 0),
+    (0, 1, 0, 128, 2, 0, 0),
+    (0, 1, 0, 128, -1, 0, 0),
     (0, 1, 0, 128, 1, 0, 0),
-    (0, 1, 0, 128, -1, 0, 0),
     (0, 1, 0, 128, 0, 0, 1),
     0,
-    (-3, 0, 0, 128, 0, 1, 0),
     (3, 0, 0, 128, -1, 0, 0),
     (3, 0, 0, 128, 0, 1, 0),
+    (3, 0, 0, 128, 0, 0, 1),
+    (1, 0, 0, 128, -1, 0, 0),
+    (1, 0, 0, 128, -1, 0, 1),
+    (1, 0, 0, 128, 0, 0, 1),
+    (-3, 0, 0, 128, 0, 1, 0),
+    (-3, 0, 0, 128, 0, 1, 1),
     (-3, 0, 0, 128, 0, 0, 1),
-    (3, 0, 0, 128, 0, 0, 1),
-    (-2, 0, 0, 128, 0, 1, 0),
-    (-2, 0, 0, 128, 0, 0, 1),
-    (2, 0, 0, 128, 0, 0, 1),
+    (-1, 0, 0, 128, 1, 0, 0),
+    (-1, 0, 0, 128, 1, 0, 1),
+    "settle",
     (-1, 0, 0, 128, 0, 0, 1),
-    (1, 0, 0, 128, 0, 0, 1),
-    "settle",
     (2, 1, 0, 128, 0, 0, 1),
-    (-3, 1, 0, 128, 0, 0, 1),
     (1, 1, 0, 128, 0, 0, 1),
     (3, 1, 0, 128, 0, 0, 1),
+    "settle",
     (4, 0, 0, 128, 0, 0, 1),
+    (4, 1, 0, 128, 0, 0, 1),
+    (-2, 1, 0, 128, 0, 0, 1),
+    1,
+    (-1, 1, 0, 128, 0, 0, 1),
+    3,
     2,
-    "settle",
-    (-1, 1, 0, 128, 0, 0, 1),
-    (-2, 1, 0, 128, 0, 0, 1),
+    4,
     -3,
-    1,
-    (4, 1, 0, 128, 0, 0, 1),
-    3,
     -1,
     -2,
-    4,
 )
 
 
@@ -241,6 +242,8 @@
     ext,
     padded,
     ends,
+    query_out,
+    query_in,
     incoming,
     shard_power,
     scales,
@@ -427,11 +430,10 @@
         sums[t % 4][0] += power_re[ROWS - 1 - t] * u
         sums[t % 4][1] += power_im[ROWS - 1 - t] * u
 
-    edges = [projected[ROWS - 2 :, i * CH : i * CH + CH] for i in range(3)]
-    edges += [jnp.zeros((2, CH), F32), key[0:2], value[0:2], jnp.zeros((4, CH), F32)]
+    edges = [projected[ROWS - 2 :, i * CH : i * CH + CH] for i in (1, 2)] + [key[0:2], value[0:2]]
     ends[p.seq, pl.ds(0, MODES)] = sums[0][0] + sums[1][0] + sums[2][0] + sums[3][0]
     ends[p.seq, pl.ds(MODES, MODES)] = sums[0][1] + sums[1][1] + sums[2][1] + sums[3][1]
-    ends[p.seq, pl.ds(2 * MODES, 16)] = jnp.concatenate(edges, axis=0)
+    ends[p.seq, pl.ds(2 * MODES, 8)] = jnp.concatenate(edges, axis=0)
     here = ends.at[p.seq]
 
     def end_copy(i):
@@ -444,7 +446,18 @@
         def _():
             end_copy(i).start()
 
+    query_out[...] = projected[ROWS - 8 :, 0:CH]
+    query_copy = small(query_out, query_in, 10, ((p.seq + 1) % SEQ, p.chan))
+
+    @pl.when(p.seq < SEQ - 1)
+    def _():
+        query_copy.start()
+
     def close_state():
+        @pl.when(p.seq < SEQ - 1)
+        def _():
+            query_copy.wait_send()
+
         for i in range(1, SEQ):
 
             @pl.when(p.seq + i < SEQ)
@@ -476,6 +489,12 @@
 
     for i in range(3):
         rim[pl.ds(2 * i, 2)] = prior_rows[i].astype(F32)
+
+    @pl.when(p.seq > 0)
+    def _():
+        query_copy.wait_recv()
+        rim[pl.ds(0, 2)] = query_in[pl.ds(6, 2)]
+
     shard_re, shard_im = shard_power[0], shard_power[1]
     last_re, last_im = power_re[ROWS - 1], power_im[ROWS - 1]
     next_re, next_im = power_re[ROWS - 2], power_im[ROWS - 2]
@@ -490,13 +509,13 @@
                 def _():
                     small(theirs, theirs, 10 + i, (j, p.chan)).wait_recv()
 
-            drive0, drive1 = first_drive(ends[j, pl.ds(40, 2)], ends[j, pl.ds(42, 2)])
+            drive0, drive1 = first_drive(ends[j, pl.ds(36, 2)], ends[j, pl.ds(38, 2)])
             re, im = incoming[0], incoming[1]
             end_re = ends[j, pl.ds(0, MODES)] + last_re * drive0 + next_re * drive1
             end_im = ends[j, pl.ds(MODES, MODES)] + last_im * drive0 + next_im * drive1
             incoming[0] = shard_re * re - shard_im * im + end_re
             incoming[1] = shard_re * im + shard_im * re + end_im
-            rim[pl.ds(0, 6)] = ends[j, pl.ds(32, 6)]
+            rim[pl.ds(2, 4)] = ends[j, pl.ds(32, 4)]
 
     in_re, in_im = incoming[0], incoming[1]
     carried = []
@@ -581,7 +600,9 @@
             pltpu.VMEM((8, CH), F32),
             pltpu.VMEM((8 + ROWS, 3 * CH), F32),
             pltpu.VMEM((2 * ROWS, CH), F32),
-            pltpu.VMEM((SEQ, 2 * MODES + 16, CH), F32),
+            pltpu.VMEM((SEQ, 2 * MODES + 8, CH), F32),
+            pltpu.VMEM((8, CH), F32),
+            pltpu.VMEM((8, CH), F32),
             pltpu.VMEM((2, MODES, CH), F32),
             pltpu.VMEM((2, MODES, CH), F32),
             pltpu.VMEM((ROWS, 128), F32),

time: 45.4 us -> 45 us (level)
  Pallas kernels: 43.8 us -> 43 us
    pallas_call x1, Pallas kernels: 43.8 us -> 43 us  [body(): pl.pallas_call(kernel, out_shape=jax.ShapeDtypeStruct((ROWS, FEATS), BF16...]
where the time goes in v6:
time: 45 us; the launch traced here: 44.5 us
  Pallas kernels  43 us (96%)
  local copies, waits for them, and re-layouts  1.47 us (3%)
    pallas_call x1, Pallas kernels, body(): pl.pallas_call(kernel, out_shape=jax.ShapeDtypeStruct((ROWS, FEATS), BF16...  43 us
    unnamed x1, local copies, waits for them, and re-layouts  1.47 us

profile of v6, /device:TPU:25, one launch (start us, length us, event | category | flops | bytes accessed | tf_op | source)
XLA Modules:
  0.0 44.5 jit_solution(5121196006950430034)
XLA Ops:
  0.0 43.0 %shard_map.109 = bf16[128,256]{1,0:T(8,128)(2,1)} custom-call(bf16[128,256]{1,0:T(8,128)(2,1)} %tokens.1, bf16[256]{0:T(256)(128)(2,1)} %gain_hbm.1, bf16[3,8192,128]{2,1,0:T(8,128)(2,1)} %bitcast.7, f32[3,3,128]{2,1,0:T(4,128)} %filter_hbm.1, bf16[3,2,128]{2,1,0:T(2,128)(2,1)} %bitcast.12, f32[16,128]{1,0:T(8,128)} %bitcast.10, f32[16,128]{1,0:T(8,128)} %bitcast.11, ...), custom_call_target="tpu_custom_call" | custom-call | flops 1073741824 | bytes 9437184 | tf_op jit(solution)/shard_map/pallas_call | solution.py:575
  43.0 1.5 %copy.13 = bf16[128,256]{1,0:T(8,128)(2,1)} copy(bf16[128,256]{1,0:T(8,128)(2,1)} %shard_map.109) | data formatting | bytes 131072

commit v7 on v6

--- a/solution.py
+++ b/solution.py
@@ -38,60 +38,61 @@
 
 
 WIDE_PLAN = (
+    (0, 0, 0, 128, -2, 0, 0),
     (0, 0, 0, 128, 2, 0, 0),
-    (0, 0, 0, 128, -2, 0, 0),
+    (0, 0, 0, 128, -1, 0, 0),
     (0, 0, 0, 128, 1, 0, 0),
-    (0, 0, 0, 128, -1, 0, 0),
     (0, 0, 0, 128, 0, 1, 0),
+    (0, 0, 0, 128, 0, 1, 1),
     (0, 0, 0, 128, 0, 0, 1),
     "stats1",
+    (0, 1, 64, 64, -2, 0, 0),
+    (0, 1, 64, 64, 2, 0, 0),
     "tables",
-    (0, 1, 64, 64, 2, 0, 0),
-    (0, 1, 64, 64, -2, 0, 0),
-    (0, 1, 0, 128, 0, 0, 1),
-    (-2, 0, 32, 32, 2, 0, 0),
-    (2, 0, 0, 32, -2, 0, 0),
-    (-2, 0, 96, 32, 2, 0, 0),
-    (-2, 0, 0, 96, 1, 0, 0),
-    (2, 0, 0, 96, -1, 0, 0),
+    (2, 0, 32, 32, -2, 0, 0),
+    (-2, 0, 0, 32, 2, 0, 0),
+    (2, 0, 0, 128, -1, 0, 0),
+    (-2, 0, 0, 128, 1, 0, 0),
+    (2, 0, 0, 64, 0, 1, 0),
     (-2, 0, 0, 64, 0, 1, 0),
-    (2, 0, 0, 64, 0, 1, 0),
+    (2, 0, 0, 128, 0, 0, 1),
     (-2, 0, 0, 128, 0, 0, 1),
-    (2, 0, 0, 128, 0, 0, 1),
-    (-1, 0, 96, 32, 2, 0, 0),
     (1, 0, 64, 32, -3, 0, 0),
-    (1, 0, 96, 32, -2, 0, 0),
+    (-1, 0, 96, 32, 3, 0, 0),
+    (1, 0, 0, 128, 0, 1, 0),
     (-1, 0, 0, 128, 0, 1, 0),
     "stats2",
     "stats3",
-    (1, 0, 0, 128, 0, 1, 0),
+    (1, 0, 0, 128, 0, 0, 1),
     (-1, 0, 0, 128, 0, 0, 1),
-    (1, 0, 0, 128, 0, 0, 1),
+    (2, 1, 64, 32, -2, 0, 0),
     (-2, 1, 96, 32, 2, 0, 0),
-    (2, 1, 64, 32, -2, 0, 0),
-    (-2, 1, 0, 128, 1, 0, 0),
+    (2, 1, 32, 96, -1, 0, 0),
+    (2, 1, 32, 96, -1, 0, 1),
+    (2, 1, 0, 128, 0, 0, 1),
+    (4, 0, 0, 64, 0, 1, 0),
+    (-2, 1, 32, 96, 1, 0, 0),
+    (-2, 1, 32, 96, 1, 0, 1),
     (-2, 1, 0, 128, 0, 0, 1),
-    (4, 0, 0, 64, 0, 1, 0),
-    (2, 1, 32, 96, -1, 0, 0),
-    (2, 1, 0, 128, 0, 0, 1),
     (3, 0, 0, 32, 0, 1, 0),
+    (3, 0, 0, 32, 0, 1, 1),
+    (-3, 0, 0, 32, 0, 1, 0),
+    (-3, 0, 0, 32, 0, 1, 1),
+    (3, 0, 0, 128, 0, 0, 1),
+    (-3, 0, 0, 128, 0, 0, 1),
+    (1, 1, 0, 128, 0, 0, 1),
+    (4, 0, 0, 128, 0, 0, 1),
     (-1, 1, 0, 128, 0, 0, 1),
-    (-3, 0, 0, 128, 0, 0, 1),
-    (4, 0, 0, 128, 0, 0, 1),
-    (3, 0, 0, 128, 0, 0, 1),
-    (1, 1, 0, 128, 0, 0, 1),
     (4, 1, 0, 128, 0, 0, 1),
-    (-3, 1, 0, 128, 0, 0, 1),
-    (3, 1, 0, 128, 0, 0, 1),
     "scale",
     0,
+    2,
     -2,
-    2,
+    1,
     -1,
-    1,
+    3,
     4,
     -3,
-    3,
 )
 
 NARROW_PLAN = (
@@ -473,8 +474,6 @@
         return acc
 
     mode_out = lax.fori_loop(0, ROWS // 4, respond, jnp.zeros((ROWS, CH), F32))
-    close_spread()
-
     def first_rows(i, so_far):
         near, far = short_filter[1, i : i + 1], short_filter[2, i : i + 1]
         before = rim[pl.ds(2 * i, 2)]
@@ -548,6 +547,7 @@
     def settle():
         if not mix.settled:
             close_state()
+            close_spread()
         mix.settle(in_flight=8)
 
     mix.run(output, {"begin": begin, "settle": settle})

time: 45 us -> 45 us (level)
  no operation moved by 1% of the time
where the time goes in v7:
time: 45 us; the launch traced here: 44.9 us
  Pallas kernels  43.4 us (96%)
  local copies, waits for them, and re-layouts  1.47 us (3%)
    pallas_call x1, Pallas kernels, body(): pl.pallas_call(kernel, out_shape=jax.ShapeDtypeStruct((ROWS, FEATS), BF16...  43.4 us
    unnamed x1, local copies, waits for them, and re-layouts  1.47 us

profile of v7, /device:TPU:25, one launch (start us, length us, event | category | flops | bytes accessed | tf_op | source)
XLA Modules:
  0.0 44.9 jit_solution(4642187800357040938)
XLA Ops:
  0.0 43.4 %shard_map.109 = bf16[128,256]{1,0:T(8,128)(2,1)} custom-call(bf16[128,256]{1,0:T(8,128)(2,1)} %tokens.1, bf16[256]{0:T(256)(128)(2,1)} %gain_hbm.1, bf16[3,8192,128]{2,1,0:T(8,128)(2,1)} %bitcast.7, f32[3,3,128]{2,1,0:T(4,128)} %filter_hbm.1, bf16[3,2,128]{2,1,0:T(2,128)(2,1)} %bitcast.12, f32[16,128]{1,0:T(8,128)} %bitcast.10, f32[16,128]{1,0:T(8,128)} %bitcast.11, ...), custom_call_target="tpu_custom_call" | custom-call | flops 1073741824 | bytes 9437184 | tf_op jit(solution)/shard_map/pallas_call | solution.py:575
  43.4 1.5 %copy.13 = bf16[128,256]{1,0:T(8,128)(2,1)} copy(bf16[128,256]{1,0:T(8,128)(2,1)} %shard_map.109) | data formatting | bytes 131072
